TPU v7x, 128 devices: a whole 4x4x4 slice. The times are simulated.
128 devices in a mesh: mu: 16 (over y, z), aux: 8 (over x, core).
Axes of the slice: x: 4, y: 4, z: 4, core: 2. Of those that a mesh axis runs over, the one named last changes fastest.
Arguments:
- blocks: bfloat16 [512, 192, 4096], P('mu', 'aux'), may hold values from -0.75 to 0.75
- row_block_of_slot: int32 [512], P('mu'), may hold values from 0 to 7
- column_block_of_slot: int32 [512], P('mu'), may hold values from 0 to 127
- block_count: int32 [16], P('mu'), may hold values from 8 to 32, as said below
- occupied: bfloat16 [8192, 64], replicated, may hold values from -6 to 6
Outputs:
- exchange: float32 [8192, 8192], P('mu', 'aux')
Inputs may be any that keep to these rules, and one draw needn't show every extreme that they name: `block_count`: some index of mu has all 32 slots live.
All inputs are finite; a program needn't handle non-finite values.
Results may differ from a plain program's by a relative error of at most 0.0022.
Values may be sent and summed in bfloat16 or wider, within the bound.
No kernel may reach another device: no remote copies, remote signals or barrier semaphores. Data moves between devices by JAX's collectives and lax.ppermute only.
A program may use at most 128 MiB of HBM per device.

v0:
```python
import jax
import jax.numpy as jnp
from jax import lax
from jax.sharding import PartitionSpec as P

BLOCK_WIDTH = 64
MB_DEV = 8


def body(blocks, row_block_of_slot, column_block_of_slot, block_count, occupied):
    number_of_slots = blocks.shape[0]
    aux_per_shard = blocks.shape[1]
    occ = occupied.shape[1]
    total_rows = occupied.shape[0]
    slot_offsets = jnp.arange(number_of_slots, dtype=jnp.int32)
    live = slot_offsets < block_count[0]
    block_tiles = blocks.reshape(number_of_slots, aux_per_shard, BLOCK_WIDTH, BLOCK_WIDTH)
    block_tiles = jnp.where(live[:, None, None, None], block_tiles, jnp.zeros_like(block_tiles))
    coeff = occupied.reshape(total_rows // BLOCK_WIDTH, BLOCK_WIDTH, occ)[column_block_of_slot]
    prods = jnp.einsum("spab,sbi->spai", block_tiles, coeff, preferred_element_type=jnp.float32)
    onehot = (row_block_of_slot[None, :] == jnp.arange(MB_DEV, dtype=jnp.int32)[:, None]).astype(
        jnp.float32
    )
    summed = jnp.einsum("ms,spai->mapi", onehot, prods, precision=lax.Precision.HIGHEST)
    local = summed.reshape(MB_DEV * BLOCK_WIDTH, aux_per_shard * occ).astype(jnp.bfloat16)
    factor = 1.0 / jnp.sqrt(jnp.float32(aux_per_shard * lax.axis_size("aux") * occ))
    partial_rows = lax.dot_general(
        local,
        lax.all_gather(local, "mu", axis=0, tiled=True),
        (((1,), (1,)), ((), ())),
        preferred_element_type=jnp.float32,
    )
    block_out = lax.psum_scatter(partial_rows, "aux", scatter_dimension=1, tiled=True)
    return block_out * factor


def solution(mesh):
    return jax.shard_map(
        body,
        mesh=mesh,
        in_specs=(P("mu", "aux", None), P("mu"), P("mu"), P("mu"), P()),
        out_specs=P("mu", "aux"),
        check_vma=False,
    )
```

profile of v0, /device:TPU:1, one launch (start us, length us, event | category | flops | bytes accessed | tf_op | source)
XLA Modules:
  0.0 355.8 jit_solution(16819102278634399539)
XLA Ops:
  6.5 0.0 all-gather.2.cloned.1.call-start
  7.2 0.7 compare_select_fusion
  7.9 2.0 copy.11
  9.9 17.9 %reshape.13 = bf16[32,24,64,64]{3,2,1,0:T(8,128)(2,1)} reshape(bf16[32,24,4096]{2,1,0:T(8,128)(2,1)} %param.5) | data formatting | bytes 12582912 | tf_op jit(solution)/shard_map/reshape | solution.py:17
  27.8 0.6 gather_fusion
  28.5 0.0 copy-start
  28.5 12.9 %fusion.2 = f32[32,24,64,64]{3,2,1,0:T(8,128)} fusion(bf16[32,24,64,64]{3,2,1,0:T(8,128)(2,1)} %reshape.13, pred[32]{0:T(512)(128)(4,1)S(1)} %iota_compare_fusion.1, bf16[32,64,64]{2,1,0:T(8,128)(2,1)S(1)} %gather_fusion), kind=kOutput, calls=%fused_computation.3 | convolution fusion | flops 405798912 | bytes 19136544 | tf_op jit(solution)/shard_map/spab,sbi->spai/dot_general | solution.py:20
  41.4 0.0 copy-done
  41.4 29.9 %convert_bitcast_fusion = bf16[8,64,24,64]{3,0,1,2:T(8,128)(2,1)S(1)} fusion(f32[32,24,64,64]{3,2,1,0:T(8,128)} %fusion.2, s32[32]{0:T(128)S(1)} %copy-done), kind=kOutput, calls=%fused_computation.7 | convolution fusion | flops 302776576 | bytes 14155904 | tf_op jit(solution)/shard_map/ms,spai->mapi/dot_general | solution.py:24
  71.2 2.0 copy.7
  73.3 2.9 convert_element_type.12
  76.2 0.0 all-gather.2.cloned.1.call-update
  76.2 0.0 reduce-scatter.2.cloned.1.call-start
  76.3 157.6 %all-gather.2.cloned.1.call-done = bf16[8192,1536]{1,0:T(8,128)(2,1)} async-done(((bf16[512,1536]{1,0:T(8,128)(2,1)}), bf16[8192,1536]{1,0:T(8,128)(2,1)}) %all-gather.2.cloned.1.call-update) | async-done | bytes 25165840 | tf_op jit(solution)/shard_map/all_gather | solution.py:29
  233.9 20.8 %fusion.13 = f32[512,8192]{1,0:T(8,128)} fusion(bf16[512,1536]{1,0:T(8,128)(2,1)} %convert_element_type.12, bf16[8192,1536]{1,0:T(8,128)(2,1)} %all-gather.2.cloned.1.call-done), kind=kOutput, calls=%fused_computation.17 | convolution fusion | flops 12884901888 | bytes 43515904 | tf_op jit(solution)/shard_map/dot_general | solution.py:27
  254.7 0.0 reduce-scatter.2.cloned.1.call-update
  254.7 90.9 %reduce-scatter.2.cloned.1.call-done = f32[512,1024]{1,0:T(8,128)} async-done(((f32[512,8192]{1,0:T(8,128)}), f32[512,1024]{1,0:T(8,128)}) %reduce-scatter.2.cloned.1.call-update) | async-done | bytes 2097168 | tf_op jit(solution)/shard_map/reduce_scatter | solution.py:33
  345.6 3.3 broadcast_multiply_fusion
  (2 shorter events, 0.0 us)
Async XLA Ops:
  6.5 227.4 %all-gather.2.cloned.1.call-start = ((), (), s32[]{:S(2)}) async-start(), calls=%async_computation.1 | async-start | bytes 26738688 | tf_op jit(solution)/shard_map/all_gather | solution.py:29
  28.5 12.9 %copy-start = (s32[32]{0:T(128)S(1)}, s32[32]{0:T(128)}, u32[]{:S(2)}) copy-start(s32[32]{0:T(128)} %param.6) | copy-start | bytes 388
  76.2 269.4 %reduce-scatter.2.cloned.1.call-start = ((), (), s32[]{:S(2)}) async-start(), calls=%async_computation.2 | async-start | bytes 18874368 | tf_op jit(solution)/shard_map/reduce_scatter | solution.py:33
Sparse Core Ops, SparseCore 0:
  76.4 157.5 all-gather.1
  254.8 90.7 reduce-scatter.1
where the time goes:
time: 356 us
  waiting for transfers between devices  249 us (70%)
  matrix products  63.5 us (18%)
  local copies, waits for them, and re-layouts  25.6 us (7%)
  between operations  14.1 us (4%)
  other arithmetic  3.97 us (1%)
    all_gather x1, waiting for transfers between devices, body(): lax.all_gather(local, 'mu', axis=0, tiled=True)  158 us
    reduce_scatter x1, waiting for transfers between devices, body(): lax.psum_scatter(partial_rows, 'aux', scatter_dimension=1, tiled=True)  90.9 us
    dot_general x1, matrix products, body(): jnp.einsum('ms,spai->mapi', onehot, prods, precision=lax.Precision.HIGHEST)  29.9 us
    dot_general x1, matrix products, body(): lax.dot_general(local, lax.all_gather(local, 'mu', axis=0, tiled=True), (...  20.8 us
    reshape x1, local copies, waits for them, and re-layouts, body(): blocks.reshape(number_of_slots, aux_per_shard, BLOCK_WIDTH, BLOCK_WIDTH)  17.9 us
    dot_general x1, matrix products, body(): jnp.einsum('spab,sbi->spai', block_tiles, coeff, preferred_element_type=j...  12.9 us
  transfers between devices with their start and end apart: 2, of which 2 were waited for; matrix products, arithmetic and copies ran while one was open for 0% of the time, Pallas kernels for 0%

commit v1 on v0

v1 whole, which is shorter than its diff:
```python
import jax
import jax.numpy as jnp
from jax import lax
from jax.experimental import pallas as pl
from jax.experimental.pallas import tpu as pltpu
from jax.sharding import PartitionSpec as P

W = 64
CHUNKS = (512,)
AXES = ("mu", "aux")
VMEM = 56 * 1024 * 1024


def device_index(y, z, x, c):
    return ((y % 4) * 4 + z % 4) * 8 + (x % 4) * 2 + c % 2


def permute(a, move):
    pairs = []
    for y in range(4):
        for z in range(4):
            for x in range(4):
                for c in range(2):
                    pairs.append((device_index(y, z, x, c), device_index(*move(y, z, x, c))))
    return lax.ppermute(a, AXES, pairs)


def strips(k):
    o, r = sum(CHUNKS[:k]), CHUNKS[k]
    out, at = [], 0
    for j in range((o + r) // 128):
        out.append((o, r, j * 128, at))
        at += r
    for j in range(r // 128 if o else 0):
        out.append((0, o, o + j * 128, at))
        at += o
    return out, at


def half_kernel(rows_ref, cols_ref, count_ref, blocks_ref, occ_ref, *refs):
    outs, (acc, turn) = refs[: len(CHUNKS)], refs[len(CHUNKS):]
    step = pl.program_id(0)
    per, naux, wide = blocks_ref.shape
    tiles = wide // 128

    @pl.when(step == 0)
    def _():
        acc[...] = jnp.zeros_like(acc)

    lane = lax.broadcasted_iota(jnp.int32, (W, 128), 1)

    @pl.loop(0, per)
    def _(j):
        s = step * per + j

        @pl.when(s < count_ref[0])
        def _():
            col = cols_ref[s]
            pair = occ_ref[:, pl.ds(pl.multiple_of(lax.shift_right_logical(col, 1) * 128, 128), 128)]
            pair = pair.astype(jnp.float32)
            other = pltpu.roll(pair, 64, 1)
            odd = (col & 1) == 1
            left = jnp.where(odd, other, pair)
            right = jnp.where(odd, pair, other)
            coeff = jnp.concatenate(
                [jnp.where(lane < 64, left, 0.0), jnp.where(lane < 64, 0.0, right)], axis=0
            ).astype(jnp.bfloat16)
            x = blocks_ref[j].astype(jnp.float32)
            x = jnp.concatenate([x[:, t * 128:(t + 1) * 128] for t in range(tiles)], axis=0)
            prod = lax.dot_general(
                x.astype(jnp.bfloat16), coeff, (((1,), (1,)), ((), ())), preferred_element_type=jnp.float32
            )
            acc[rows_ref[s]] += prod

    @pl.when(step == pl.num_programs(0) - 1)
    def _():
        low = lax.broadcasted_iota(jnp.int32, (tiles, 128), 1) < 64
        at = 0
        for k, r in enumerate(CHUNKS):
            for b in range(r // W):
                m = at // W + b
                for q in range(naux // 2):
                    even = acc[m, pl.ds(2 * q, tiles, stride=naux), :]
                    odd = acc[m, pl.ds(2 * q + 1, tiles, stride=naux), :]
                    turn[pl.ds(0, tiles, stride=2), :] = jnp.where(low, even, pltpu.roll(odd, 64, 1))
                    turn[pl.ds(1, tiles, stride=2), :] = jnp.where(low, pltpu.roll(even, 64, 1), odd)
                    outs[k][b * W:(b + 1) * W, q * 128:(q + 1) * 128] = turn[...].astype(jnp.bfloat16)
            at += r


def half_rows(blocks, rows, cols, count, occ_t):
    slots, naux, wide = blocks.shape
    per = slots // 4
    wide_out = naux * W
    return pl.pallas_call(
        half_kernel,
        grid_spec=pltpu.PrefetchScalarGridSpec(
            num_scalar_prefetch=3,
            grid=(slots // per,),
            in_specs=[
                pl.BlockSpec((per, naux, wide), lambda i, *_: (i, 0, 0)),
                pl.BlockSpec(occ_t.shape, lambda i, *_: (0, 0)),
            ],
            out_specs=[pl.BlockSpec((r, wide_out), lambda i, *_: (0, 0)) for r in CHUNKS],
            scratch_shapes=[
                pltpu.VMEM((8, naux * wide // 128, 128), jnp.float32),
                pltpu.VMEM((W, 128), jnp.float32),
            ],
        ),
        out_shape=[jax.ShapeDtypeStruct((r, wide_out), jnp.bfloat16) for r in CHUNKS],
        compiler_params=pltpu.CompilerParams(vmem_limit_bytes=VMEM),
        cost_estimate=pl.CostEstimate(flops=2 * 10**9, bytes_accessed=8 * 10**6, transcendentals=0),
        name="half_rows",
    )(rows, cols, count, blocks, occ_t)


def product_kernel(k, place_ref, *refs):
    pieces = [4 if r is None else r for r in ()]
    n = (k + 1) * 5
    i_refs, j_refs = refs[:n], refs[n:2 * n]
    mine, theirs = refs[2 * n], refs[2 * n + 1]
    iv, jv, ob, in_sem, out_sem = refs[2 * n + 2:]
    core, y = place_ref[0], place_ref[1]
    o, r = sum(CHUNKS[:k]), CHUNKS[k]
    copies = []
    for side, (srcs, dst) in enumerate(((i_refs, iv), (j_refs, jv))):
        at = 0
        for m in range(k + 1):
            h = CHUNKS[m]
            own, plus, minus, two_a, two_b = srcs[5 * m:5 * m + 5]
            for src, where in (
                (own, dst.at[0, pl.ds(at, h)]),
                (plus, dst.at[1, pl.ds(at, h)]),
                (minus, dst.at[3, pl.ds(at, h)]),
                (two_a, dst.at[2, pl.ds(at, h // 2)]),
                (two_b, dst.at[2, pl.ds(at + h // 2, h // 2)]),
            ):
                copy = pltpu.make_async_copy(src, where, in_sem.at[side, len(copies) % n])
                copy.start()
                copies.append(copy)
            at += h
    for copy in copies:
        copy.wait()
    plan, _ = strips(k)

    @pl.loop(0, 16)
    def _(t):
        dz, dy = lax.shift_right_logical(t, 2), t & 3
        nt = (((1,), (1,)), ((), ()))
        first = lax.dot_general(
            iv[dz, o:o + r, :], jv[dy, 0:o + r, :], nt, preferred_element_type=jnp.float32
        )
        for (row, rows, col, at) in plan:
            if row == o:
                ob[dz, dy, at:at + rows, :] = first[:, col:col + 128]
        if o:
            second = lax.dot_general(
                iv[dz, 0:o, :], jv[dy, o:o + r, :], nt, preferred_element_type=jnp.float32
            )
            for (row, rows, col, at) in plan:
                if row != o:
                    ob[dz, dy, at:at + rows, :] = second[:, col - o:col - o + 128]
        target = (y + dy) & 3
        e = dz & 1

        @pl.when(lax.shift_right_logical(dz, 1) == core)
        def _():
            pltpu.make_async_copy(ob.at[dz, dy], mine.at[target, e], out_sem.at[dz, dy]).start()

        @pl.when(lax.shift_right_logical(dz, 1) != core)
        def _():
            pltpu.make_async_copy(ob.at[dz, dy], theirs.at[target, e], out_sem.at[dz, dy]).start()

    @pl.loop(0, 16)
    def _(t):
        dz, dy = lax.shift_right_logical(t, 2), t & 3
        pltpu.make_async_copy(ob.at[dz, dy], mine.at[0, 0], out_sem.at[dz, dy]).wait()


def product(k, place, i_pieces, j_pieces):
    _, size = strips(k)
    upto = sum(CHUNKS[:k + 1])
    depth = i_pieces[0].shape[1]
    n = (k + 1) * 5
    shape = jax.ShapeDtypeStruct((4, 2, size, 128), jnp.float32)
    return pl.pallas_call(
        lambda *refs: product_kernel(k, *refs),
        grid_spec=pltpu.PrefetchScalarGridSpec(
            num_scalar_prefetch=1,
            grid=(1,),
            in_specs=[pl.BlockSpec(memory_space=pl.ANY)] * (2 * n),
            out_specs=[pl.BlockSpec(memory_space=pl.ANY)] * 2,
            scratch_shapes=[
                pltpu.VMEM((4, upto, depth), jnp.bfloat16),
                pltpu.VMEM((4, upto, depth), jnp.bfloat16),
                pltpu.VMEM((4, 4, size, 128), jnp.float32),
                pltpu.SemaphoreType.DMA((2, n)),
                pltpu.SemaphoreType.DMA((4, 4)),
            ],
        ),
        out_shape=[shape, shape],
        compiler_params=pltpu.CompilerParams(vmem_limit_bytes=VMEM),
        cost_estimate=pl.CostEstimate(
            flops=2 * 16 * size * 128 * depth, bytes_accessed=16 * size * 512 + 16 * upto * depth, transcendentals=0
        ),
        name="product",
    )(place, *i_pieces, *j_pieces)


def core_kernel(place_ref, mine, other, rounded, own):
    total = mine[...] + other[...]
    rounded[...] = total.astype(jnp.bfloat16)

    @pl.when(pl.program_id(0) == place_ref[2])
    def _():
        own[...] = total[0]


def core_sum(place, mine, other):
    _, two, size, _ = mine.shape
    block = pl.BlockSpec((1, two, size, 128), lambda i, *_: (i, 0, 0, 0))
    return pl.pallas_call(
        core_kernel,
        grid_spec=pltpu.PrefetchScalarGridSpec(
            num_scalar_prefetch=1,
            grid=(4,),
            in_specs=[block, block],
            out_specs=[block, pl.BlockSpec((two, size, 128), lambda i, *_: (0, 0, 0))],
        ),
        out_shape=[
            jax.ShapeDtypeStruct(mine.shape, jnp.bfloat16),
            jax.ShapeDtypeStruct(mine.shape[1:], jnp.float32),
        ],
        compiler_params=pltpu.CompilerParams(vmem_limit_bytes=VMEM),
        cost_estimate=pl.CostEstimate(flops=mine.size, bytes_accessed=11 * mine.size, transcendentals=0),
        name="core_sum",
    )(place, mine, other)


def aux_kernel(place_ref, scale_ref, parts, own, first, second):
    x = place_ref[2]
    for e, out in ((0, first), (1, second)):
        total = own[e]
        for j in range(1, 4):
            total = total + parts[(x + j) & 3, e].astype(jnp.float32)
        out[...] = total * scale_ref[0]


def aux_sum(place, scale, parts, own):
    _, two, size, _ = parts.shape
    steps = 4
    part = size // steps
    shape = jax.ShapeDtypeStruct((size, 128), jnp.float32)
    return pl.pallas_call(
        aux_kernel,
        grid_spec=pltpu.PrefetchScalarGridSpec(
            num_scalar_prefetch=2,
            grid=(steps,),
            in_specs=[
                pl.BlockSpec((4, two, part, 128), lambda i, *_: (0, 0, i, 0)),
                pl.BlockSpec((two, part, 128), lambda i, *_: (0, i, 0)),
            ],
            out_specs=[pl.BlockSpec((part, 128), lambda i, *_: (i, 0))] * 2,
        ),
        out_shape=[shape, shape],
        compiler_params=pltpu.CompilerParams(vmem_limit_bytes=VMEM),
        cost_estimate=pl.CostEstimate(flops=parts.size, bytes_accessed=5 * parts.size, transcendentals=0),
        name="aux_sum",
    )(place, scale, parts, own)


def place_kernel(place_ref, *refs):
    out = refs[-1]
    half = place_ref[3]
    for k in range(len(CHUNKS)):
        for n in range(2):
            base = (half if n == 0 else 1 - half) * 512
            for (row, rows, col, at) in strips(k)[0]:
                out[row:row + rows, pl.ds(pl.multiple_of(base + col, 128), 128)] = refs[2 * k + n][at:at + rows, :]


def assemble(place, pieces):
    return pl.pallas_call(
        place_kernel,
        grid_spec=pltpu.PrefetchScalarGridSpec(
            num_scalar_prefetch=1,
            grid=(1,),
            in_specs=[pl.BlockSpec(p.shape, lambda i, *_: (0, 0)) for p in pieces],
            out_specs=pl.BlockSpec((512, 1024), lambda i, *_: (0, 0)),
        ),
        out_shape=jax.ShapeDtypeStruct((512, 1024), jnp.float32),
        compiler_params=pltpu.CompilerParams(vmem_limit_bytes=VMEM),
        name="assemble",
    )(place, *pieces)


def gather(h, plus, minus):
    half = h.shape[0] // 2
    from_below, from_above = permute(h, plus), permute(h, minus)
    two_a = permute(from_below[:half], plus)
    two_b = permute(from_above[half:], minus)
    return [h, from_above, from_below, two_a, two_b]


def body(blocks, row_block_of_slot, column_block_of_slot, block_count, occupied):
    mu, aux = lax.axis_index("mu"), lax.axis_index("aux")
    y, z, x, c = mu // 4, mu % 4, aux // 2, aux % 2
    place = jnp.stack([c, y, x, z % 2]).astype(jnp.int32)
    total_aux = blocks.shape[1] * lax.axis_size("aux") * occupied.shape[1]
    scale = (1.0 / jnp.sqrt(jnp.float32(total_aux))).reshape(1)
    halves = half_rows(blocks, row_block_of_slot, column_block_of_slot, block_count, occupied.T)
    i_pieces, j_pieces, done = [], [], []
    groups = [[2 * g + core for g in range(4)] for core in range(2)]
    for k, h in enumerate(halves):
        i_pieces += gather(h, lambda y, z, x, c: (y, z + 1, x, c), lambda y, z, x, c: (y, z - 1, x, c))
        j_pieces += gather(h, lambda y, z, x, c: (y + 1, z, x, c), lambda y, z, x, c: (y - 1, z, x, c))
        mine, theirs = product(k, place, list(i_pieces), list(j_pieces))
        other = permute(theirs, lambda y, z, x, c: (y, z, x, 1 - c))
        rounded, own = core_sum(place, mine, other)
        parts = lax.all_to_all(rounded, "aux", 0, 0, tiled=True, axis_index_groups=groups)
        first, second = aux_sum(place, scale, parts, own)
        done.append(permute(first, lambda y, z, x, c: (y, z + 2 * c, x, z // 2)))
        done.append(permute(second, lambda y, z, x, c: (y, z + 2 * c + 1, x, z // 2)))
    return assemble(place, done)


def solution(mesh):
    return jax.shard_map(
        body,
        mesh=mesh,
        in_specs=(P("mu", "aux", None), P("mu"), P("mu"), P("mu"), P()),
        out_specs=P("mu", "aux"),
        check_vma=False,
    )
```

time: 356 us -> 216 us (0.61)
  waiting for transfers between devices: 249 us -> 82 us
  matrix products: 63.5 us -> 0 us
  blocking collectives: 0 us -> 54.2 us
  Pallas kernels: 0 us -> 51.3 us
  starting transfers between devices: 0.04 us -> 25.9 us
  local copies, waits for them, and re-layouts: 25.6 us -> 1.21 us
  between operations: 14.1 us -> 0.74 us
    all_gather x1 -> x0, waiting for transfers between devices: 158 us -> none  [body(): lax.all_gather(local, 'mu', axis=0, tiled=True)]
    reduce_scatter x1 -> x0, waiting for transfers between devices: 90.9 us -> none  [body(): lax.psum_scatter(partial_rows, 'aux', scatter_dimension=1, tiled=True)]
    ppermute x0 -> x11, waiting for transfers between devices: none -> 82 us  [permute(): return lax.ppermute(a, AXES, pairs)]
    dot_general x3 -> x0, matrix products: 63.5 us -> none  [the longest x1 29.9 us: body(): jnp.einsum('ms,spai->mapi', onehot, prods, precision=lax.Precision.HIGHEST)]
    all_to_all x0 -> x1, blocking collectives: none -> 54.2 us  [body(): lax.all_to_all(rounded, 'aux', 0, 0, tiled=True, axis_index_groups=groups)]
    pallas_call x0 -> x5, Pallas kernels: none -> 51.3 us  [the longest x1 22.6 us: product(): pl.pallas_call(lambda *refs: product_kernel(k, *refs), grid_spec=pltpu.Pr...]
    ppermute x0 -> x11, starting transfers between devices: none -> 25.9 us  [permute(): return lax.ppermute(a, AXES, pairs)]
    reshape x2 -> x0, local copies, waits for them, and re-layouts: 20 us -> none  [the longest x1 17.9 us: body(): blocks.reshape(number_of_slots, aux_per_shard, BLOCK_WIDTH, BLOCK_WIDTH)]
  transfers between devices with their start and end apart: 2 -> 11, of which waited for: 2 -> 8; matrix products, arithmetic and copies ran while one was open for 0% -> 0% of each run, Pallas kernels for 0% -> 0%
where the time goes in v1:
time: 216 us
  waiting for transfers between devices  82 us (38%)
  blocking collectives  54.2 us (25%)
  Pallas kernels  51.3 us (24%)
  starting transfers between devices  25.9 us (12%)
    ppermute x11, waiting for transfers between devices, permute(): return lax.ppermute(a, AXES, pairs)  82 us
    all_to_all x1, blocking collectives, body(): lax.all_to_all(rounded, 'aux', 0, 0, tiled=True, axis_index_groups=groups)  54.2 us
    ppermute x11, starting transfers between devices, permute(): return lax.ppermute(a, AXES, pairs)  25.9 us
    pallas_call x1, Pallas kernels, product(): pl.pallas_call(lambda *refs: product_kernel(k, *refs), grid_spec=pltpu.Pr...  22.6 us
    pallas_call x1, Pallas kernels, half_rows(): pl.pallas_call(half_kernel, grid_spec=pltpu.PrefetchScalarGridSpec(num_sc...  10.2 us
    pallas_call x1, Pallas kernels, core_sum(): pl.pallas_call(core_kernel, grid_spec=pltpu.PrefetchScalarGridSpec(num_sc...  9.46 us
    pallas_call x1, Pallas kernels, aux_sum(): pl.pallas_call(aux_kernel, grid_spec=pltpu.PrefetchScalarGridSpec(num_sca...  5.26 us
  transfers between devices with their start and end apart: 11, of which 8 were waited for; matrix products, arithmetic and copies ran while one was open for 0% of the time, Pallas kernels for 0%

profile of v1, /device:TPU:1, one launch (start us, length us, event | category | flops | bytes accessed | tf_op | source)
XLA Modules:
  0.0 216.0 jit_solution(11029565060961181049)
XLA Ops:
  0.7 10.2 %half_rows.1.refs_1_.refs_6_ = bf16[512,1536]{1,0:T(8,128)(2,1)} custom-call(s32[32]{0:T(128)} %rows_ref.1, s32[32]{0:T(128)} %cols_ref.1, s32[1]{0:T(128)S(6)} %copy.6.count_ref, bf16[32,24,4096]{2,1,0:T(8,128)(2,1)} %blocks_ref.1, bf16[64,8192]{1,0:T(8,128)(2,1)} %bitcast.5), custom_call_target="tpu_custom_call" | custom-call | flops 2000000000 | bytes 8000000 | tf_op jit(solution)/shard_map/half_rows/pallas_call | solution.py:95
  10.9 6.2 %collective-permute-start.5 = (bf16[512,1536]{1,0:T(8,128)(2,1)}, bf16[512,1536]{1,0:T(8,128)(2,1)S(1)}, u32[]{:S(2)}, u32[]{:S(2)}) collective-permute-start(bf16[512,1536]{1,0:T(8,128)(2,1)} %half_rows.1.refs_1_.refs_6_), channel_id=1, source_target_pairs={{0,32},{1,33},{2,34},{3,35},{4,36},{5,37},{6,38},{7,39},{8,40},{9,... | collective-permute-start | bytes 4718600 | tf_op jit(solution)/shard_map/ppermute | solution.py:25
  17.1 0.0 collective-permute-start.4
  17.1 1.1 collective-permute-start.1
  18.2 3.2 %collective-permute-start = (bf16[512,1536]{1,0:T(8,128)(2,1)}, bf16[512,1536]{1,0:T(8,128)(2,1)S(1)}, u32[]{:S(2)}, u32[]{:S(2)}) collective-permute-start(bf16[512,1536]{1,0:T(8,128)(2,1)} %half_rows.1.refs_1_.refs_6_), channel_id=1, source_target_pairs={{0,24},{1,25},{2,26},{3,27},{4,28},{5,29},{6,30},{7,31},{8,0},{9,1... | collective-permute-start | bytes 4718600 | tf_op jit(solution)/shard_map/ppermute | solution.py:25
  21.4 29.0 %collective-permute-done.5.refs_8_ = bf16[512,1536]{1,0:T(8,128)(2,1)S(1)} collective-permute-done((bf16[512,1536]{1,0:T(8,128)(2,1)}, bf16[512,1536]{1,0:T(8,128)(2,1)S(1)}, u32[]{:S(2)}, u32[]{:S(2)}) %collective-permute-start.5) | collective-permute-done | bytes 1572896 | tf_op jit(solution)/shard_map/ppermute | solution.py:25
  50.4 0.0 copy-start.2
  50.4 0.1 slice.18
  50.5 2.2 %collective-permute-start.6 = (bf16[256,1536]{1,0:T(8,128)(2,1)S(1)}, bf16[256,1536]{1,0:T(8,128)(2,1)}, u32[]{:S(2)}, u32[]{:S(2)}) collective-permute-start(bf16[256,1536]{1,0:T(8,128)(2,1)S(1)} %slice.18), channel_id=1, source_target_pairs={{0,32},{1,33},{2,34},{3,35},{4,36},{5,37},{6,38},{7,39},{8,40},{9,... | collective-permute-start | bytes 2359304 | tf_op jit(solution)/shard_map/ppermute | solution.py:25
  52.7 0.0 collective-permute-done.4.refs_7_
  52.7 0.0 copy-start.3
  52.7 0.1 slice.19
  52.7 1.2 collective-permute-start.7
  53.9 1.2 collective-permute-done.1.refs_3_
  55.1 0.0 copy-start.4
  55.1 0.1 slice.16
  55.2 0.0 copy-done.2
  55.2 0.1 collective-permute-start.2
  55.3 0.0 collective-permute-done.refs_2_
  55.3 0.0 copy-start.5
  55.3 0.1 slice.17
  55.3 0.0 copy-done.3
  55.4 3.3 %collective-permute-start.3 = (bf16[256,1536]{1,0:T(8,128)(2,1)S(1)}, bf16[256,1536]{1,0:T(8,128)(2,1)}, u32[]{:S(2)}, u32[]{:S(2)}) collective-permute-start(bf16[256,1536]{1,0:T(8,128)(2,1)S(1)} %slice.17), channel_id=1, source_target_pairs={{0,24},{1,25},{2,26},{3,27},{4,28},{5,29},{6,30},{7,31},{8,0},{9,1... | collective-permute-start | bytes 2359304 | tf_op jit(solution)/shard_map/ppermute | solution.py:25
  58.6 0.0 copy-done.4
  58.6 0.0 copy-done.5
  58.6 0.6 pad_add_fusion.refs_0_.place_ref
  59.2 10.1 %collective-permute-done.6.refs_9_ = bf16[256,1536]{1,0:T(8,128)(2,1)} collective-permute-done((bf16[256,1536]{1,0:T(8,128)(2,1)S(1)}, bf16[256,1536]{1,0:T(8,128)(2,1)}, u32[]{:S(2)}, u32[]{:S(2)}) %collective-permute-start.6) | collective-permute-done | bytes 786464 | tf_op jit(solution)/shard_map/ppermute | solution.py:25
  69.4 0.7 collective-permute-done.7.refs_10_
  70.1 4.2 %collective-permute-done.2.refs_4_ = bf16[256,1536]{1,0:T(8,128)(2,1)} collective-permute-done((bf16[256,1536]{1,0:T(8,128)(2,1)S(1)}, bf16[256,1536]{1,0:T(8,128)(2,1)}, u32[]{:S(2)}, u32[]{:S(2)}) %collective-permute-start.2) | collective-permute-done | bytes 786464 | tf_op jit(solution)/shard_map/ppermute | solution.py:25
  74.3 0.0 collective-permute-done.3.refs_5_
  74.3 22.6 %product.1 = (f32[4,2,2048,128]{3,2,1,0:T(8,128)}, f32[4,2,2048,128]{3,2,1,0:T(8,128)}) custom-call(s32[4]{0:T(128)} %pad_add_fusion.refs_0_.place_ref, bf16[512,1536]{1,0:T(8,128)(2,1)} %half_rows.1.refs_1_.refs_6_, bf16[512,1536]{1,0:T(8,128)(2,1)} %copy-done.5, bf16[512,1536]{1,0:T(8,128)(2,1)} %copy-done.4, ...), custom_call_target="tpu_custom_call" | custom-call | flops 12884901888 | bytes 29360128 | tf_op jit(solution)/shard_map/product/pallas_call | solution.py:186
  96.9 2.8 %collective-permute-start.8 = (f32[4,2,2048,128]{3,2,1,0:T(8,128)}, f32[4,2,2048,128]{3,2,1,0:T(8,128)}, u32[]{:S(2)}, u32[]{:S(2)}) collective-permute-start(f32[4,2,2048,128]{3,2,1,0:T(8,128)} %get-tuple-element.12), channel_id=1, source_target_pairs={{0,1},{1,0},{2,3},{3,2},{4,5},{5,4},{6,7},{7,6},{8,9},{9,8},{10,11... | collective-permute-start | bytes 25165832 | tf_op jit(solution)/shard_map/ppermute | solution.py:25
  99.7 13.1 %collective-permute-done.8.other = f32[4,2,2048,128]{3,2,1,0:T(8,128)} collective-permute-done((f32[4,2,2048,128]{3,2,1,0:T(8,128)}, f32[4,2,2048,128]{3,2,1,0:T(8,128)}, u32[]{:S(2)}, u32[]{:S(2)}) %collective-permute-start.8) | collective-permute-done | bytes 8388640 | tf_op jit(solution)/shard_map/ppermute | solution.py:25
  112.8 9.5 %core_sum.1 = (bf16[4,2,2048,128]{3,2,1,0:T(8,128)(2,1)}, f32[2,2048,128]{2,1,0:T(8,128)}) custom-call(s32[4]{0:T(128)} %pad_add_fusion.refs_0_.place_ref, f32[4,2,2048,128]{3,2,1,0:T(8,128)} %get-tuple-element.11.mine, f32[4,2,2048,128]{3,2,1,0:T(8,128)} %collective-permute-done.8.other), custom_call_target="tpu_custom_call" | custom-call | flops 2097152 | bytes 23068672 | tf_op jit(solution)/shard_map/core_sum/pallas_call | solution.py:222
  122.3 54.2 %all_to_all.5.parts = bf16[4,2,2048,128]{3,2,1,0:T(8,128)(2,1)} all-to-all(bf16[4,2,2048,128]{3,2,1,0:T(8,128)(2,1)} %get-tuple-element.13), channel_id=1, replica_groups={{0,2,4,6},{1,3,5,7},{8,10,12,14},{9,11,13,15},{16,18,20,22},{17,19,21,2..., dimensions={0} | all-to-all | bytes 8388608 | tf_op jit(solution)/shard_map/all_to_all | solution.py:320
  176.5 5.3 %aux_sum.1 = (f32[2048,128]{1,0:T(8,128)}, f32[2048,128]{1,0:T(8,128)}) custom-call(s32[4]{0:T(128)} %pad_add_fusion.refs_0_.place_ref, f32[1]{0:T(128)} %constant.56.clone.1.scale_ref, bf16[4,2,2048,128]{3,2,1,0:T(8,128)(2,1)} %all_to_all.5.parts, f32[2,2048,128]{2,1,0:T(8,128)} %get-tuple-element.14.own), custom_call_target="tpu_custom_call" | custom-call | flops 2097152 | bytes 10485760 | tf_op jit(solution)/shard_map/aux_sum/pallas_call | solution.py:254
  181.8 5.8 %collective-permute-start.9 = (f32[2048,128]{1,0:T(8,128)}, f32[2048,128]{1,0:T(8,128)S(1)}, u32[]{:S(2)}, u32[]{:S(2)}) collective-permute-start(f32[2048,128]{1,0:T(8,128)} %get-tuple-element.15), channel_id=1, source_target_pairs={{0,0},{1,16},{2,2},{3,18},{4,4},{5,20},{6,6},{7,22},{8,8},{9,24},{... | collective-permute-start | bytes 3145736 | tf_op jit(solution)/shard_map/ppermute | solution.py:25
  187.6 0.1 collective-permute-start.10
  187.7 22.0 %collective-permute-done.9.refs_0_ = f32[2048,128]{1,0:T(8,128)S(1)} collective-permute-done((f32[2048,128]{1,0:T(8,128)}, f32[2048,128]{1,0:T(8,128)S(1)}, u32[]{:S(2)}, u32[]{:S(2)}) %collective-permute-start.9) | collective-permute-done | bytes 1048608 | tf_op jit(solution)/shard_map/ppermute | solution.py:25
  209.7 0.0 copy-start
  209.7 1.6 collective-permute-done.10.refs_1_
  211.2 0.0 copy-done
  211.2 0.0 copy-start.1
  211.2 1.0 copy-done.1
  212.2 3.8 %assemble.1 = f32[512,1024]{1,0:T(8,128)} custom-call(s32[4]{0:T(128)} %pad_add_fusion.refs_0_.place_ref, f32[2048,128]{1,0:T(8,128)} %copy-done, f32[2048,128]{1,0:T(8,128)} %copy-done.1), custom_call_target="tpu_custom_call" | custom-call | tf_op jit(solution)/shard_map/assemble/pallas_call | solution.py:283
Async XLA Ops:
  10.9 39.6 %collective-permute-start.5 = (bf16[512,1536]{1,0:T(8,128)(2,1)}, bf16[512,1536]{1,0:T(8,128)(2,1)S(1)}, u32[]{:S(2)}, u32[]{:S(2)}) collective-permute-start(bf16[512,1536]{1,0:T(8,128)(2,1)} %half_rows.1.refs_1_.refs_6_), channel_id=1, source_target_pairs={{0,32},{1,33},{2,34},{3,35},{4,36},{5,37},{6,38},{7,39},{8,40},{9,... | collective-permute-start | bytes 4718600 | tf_op jit(solution)/shard_map/ppermute | solution.py:25
  17.1 35.6 %collective-permute-start.4 = (bf16[512,1536]{1,0:T(8,128)(2,1)}, bf16[512,1536]{1,0:T(8,128)(2,1)S(1)}, u32[]{:S(2)}, u32[]{:S(2)}) collective-permute-start(bf16[512,1536]{1,0:T(8,128)(2,1)} %half_rows.1.refs_1_.refs_6_), channel_id=1, source_target_pairs={{0,96},{1,97},{2,98},{3,99},{4,100},{5,101},{6,102},{7,103},{8,104... | collective-permute-start | bytes 4718600 | tf_op jit(solution)/shard_map/ppermute | solution.py:25
  17.1 38.0 %collective-permute-start.1 = (bf16[512,1536]{1,0:T(8,128)(2,1)}, bf16[512,1536]{1,0:T(8,128)(2,1)S(1)}, u32[]{:S(2)}, u32[]{:S(2)}) collective-permute-start(bf16[512,1536]{1,0:T(8,128)(2,1)} %half_rows.1.refs_1_.refs_6_), channel_id=1, source_target_pairs={{0,8},{1,9},{2,10},{3,11},{4,12},{5,13},{6,14},{7,15},{8,16},{9,17... | collective-permute-start | bytes 4718600 | tf_op jit(solution)/shard_map/ppermute | solution.py:25
  18.2 37.1 %collective-permute-start = (bf16[512,1536]{1,0:T(8,128)(2,1)}, bf16[512,1536]{1,0:T(8,128)(2,1)S(1)}, u32[]{:S(2)}, u32[]{:S(2)}) collective-permute-start(bf16[512,1536]{1,0:T(8,128)(2,1)} %half_rows.1.refs_1_.refs_6_), channel_id=1, source_target_pairs={{0,24},{1,25},{2,26},{3,27},{4,28},{5,29},{6,30},{7,31},{8,0},{9,1... | collective-permute-start | bytes 4718600 | tf_op jit(solution)/shard_map/ppermute | solution.py:25
  50.4 4.7 %copy-start.2 = (bf16[512,1536]{1,0:T(8,128)(2,1)}, bf16[512,1536]{1,0:T(8,128)(2,1)S(1)}, u32[]{:S(2)}) copy-start(bf16[512,1536]{1,0:T(8,128)(2,1)S(1)} %collective-permute-done.5.refs_8_) | copy-start | bytes 4718596
  50.5 18.9 %collective-permute-start.6 = (bf16[256,1536]{1,0:T(8,128)(2,1)S(1)}, bf16[256,1536]{1,0:T(8,128)(2,1)}, u32[]{:S(2)}, u32[]{:S(2)}) collective-permute-start(bf16[256,1536]{1,0:T(8,128)(2,1)S(1)} %slice.18), channel_id=1, source_target_pairs={{0,32},{1,33},{2,34},{3,35},{4,36},{5,37},{6,38},{7,39},{8,40},{9,... | collective-permute-start | bytes 2359304 | tf_op jit(solution)/shard_map/ppermute | solution.py:25
  52.7 2.7 %copy-start.3 = (bf16[512,1536]{1,0:T(8,128)(2,1)}, bf16[512,1536]{1,0:T(8,128)(2,1)S(1)}, u32[]{:S(2)}) copy-start(bf16[512,1536]{1,0:T(8,128)(2,1)S(1)} %collective-permute-done.4.refs_7_) | copy-start | bytes 4718596
  52.7 17.4 %collective-permute-start.7 = (bf16[256,1536]{1,0:T(8,128)(2,1)S(1)}, bf16[256,1536]{1,0:T(8,128)(2,1)}, u32[]{:S(2)}, u32[]{:S(2)}) collective-permute-start(bf16[256,1536]{1,0:T(8,128)(2,1)S(1)} %slice.19), channel_id=1, source_target_pairs={{0,96},{1,97},{2,98},{3,99},{4,100},{5,101},{6,102},{7,103},{8,104... | collective-permute-start | bytes 2359304 | tf_op jit(solution)/shard_map/ppermute | solution.py:25
  55.1 3.5 %copy-start.4 = (bf16[512,1536]{1,0:T(8,128)(2,1)}, bf16[512,1536]{1,0:T(8,128)(2,1)S(1)}, u32[]{:S(2)}) copy-start(bf16[512,1536]{1,0:T(8,128)(2,1)S(1)} %collective-permute-done.1.refs_3_) | copy-start | bytes 4718596
  55.2 19.1 %collective-permute-start.2 = (bf16[256,1536]{1,0:T(8,128)(2,1)S(1)}, bf16[256,1536]{1,0:T(8,128)(2,1)}, u32[]{:S(2)}, u32[]{:S(2)}) collective-permute-start(bf16[256,1536]{1,0:T(8,128)(2,1)S(1)} %slice.16), channel_id=1, source_target_pairs={{0,8},{1,9},{2,10},{3,11},{4,12},{5,13},{6,14},{7,15},{8,16},{9,17... | collective-permute-start | bytes 2359304 | tf_op jit(solution)/shard_map/ppermute | solution.py:25
  55.3 3.4 %copy-start.5 = (bf16[512,1536]{1,0:T(8,128)(2,1)}, bf16[512,1536]{1,0:T(8,128)(2,1)S(1)}, u32[]{:S(2)}) copy-start(bf16[512,1536]{1,0:T(8,128)(2,1)S(1)} %collective-permute-done.refs_2_) | copy-start | bytes 4718596
  55.4 19.0 %collective-permute-start.3 = (bf16[256,1536]{1,0:T(8,128)(2,1)S(1)}, bf16[256,1536]{1,0:T(8,128)(2,1)}, u32[]{:S(2)}, u32[]{:S(2)}) collective-permute-start(bf16[256,1536]{1,0:T(8,128)(2,1)S(1)} %slice.17), channel_id=1, source_target_pairs={{0,24},{1,25},{2,26},{3,27},{4,28},{5,29},{6,30},{7,31},{8,0},{9,1... | collective-permute-start | bytes 2359304 | tf_op jit(solution)/shard_map/ppermute | solution.py:25
  96.9 15.9 %collective-permute-start.8 = (f32[4,2,2048,128]{3,2,1,0:T(8,128)}, f32[4,2,2048,128]{3,2,1,0:T(8,128)}, u32[]{:S(2)}, u32[]{:S(2)}) collective-permute-start(f32[4,2,2048,128]{3,2,1,0:T(8,128)} %get-tuple-element.12), channel_id=1, source_target_pairs={{0,1},{1,0},{2,3},{3,2},{4,5},{5,4},{6,7},{7,6},{8,9},{9,8},{10,11... | collective-permute-start | bytes 25165832 | tf_op jit(solution)/shard_map/ppermute | solution.py:25
  181.8 27.9 %collective-permute-start.9 = (f32[2048,128]{1,0:T(8,128)}, f32[2048,128]{1,0:T(8,128)S(1)}, u32[]{:S(2)}, u32[]{:S(2)}) collective-permute-start(f32[2048,128]{1,0:T(8,128)} %get-tuple-element.15), channel_id=1, source_target_pairs={{0,0},{1,16},{2,2},{3,18},{4,4},{5,20},{6,6},{7,22},{8,8},{9,24},{... | collective-permute-start | bytes 3145736 | tf_op jit(solution)/shard_map/ppermute | solution.py:25
  187.6 23.7 %collective-permute-start.10 = (f32[2048,128]{1,0:T(8,128)}, f32[2048,128]{1,0:T(8,128)S(1)}, u32[]{:S(2)}, u32[]{:S(2)}) collective-permute-start(f32[2048,128]{1,0:T(8,128)} %get-tuple-element.16), channel_id=1, source_target_pairs={{0,8},{1,24},{2,10},{3,26},{4,12},{5,28},{6,14},{7,30},{8,16},{9,0... | collective-permute-start | bytes 3145736 | tf_op jit(solution)/shard_map/ppermute | solution.py:25
  209.7 1.6 copy-start
  211.2 1.0 copy-start.1

commit v2 on v0

v2 whole, which is shorter than its diff:
```python
import jax
import jax.numpy as jnp
from jax import lax
from jax.experimental import pallas as pl
from jax.experimental.pallas import tpu as pltpu
from jax.sharding import PartitionSpec as P

W = 64
CHUNKS = (512,)
AXES = ("mu", "aux")
MIB = 1024 * 1024


def device_index(y, z, x, c):
    return ((y % 4) * 4 + z % 4) * 8 + (x % 4) * 2 + c % 2


def permute(a, move):
    pairs = []
    for y in range(4):
        for z in range(4):
            for x in range(4):
                for c in range(2):
                    pairs.append((device_index(y, z, x, c), device_index(*move(y, z, x, c))))
    return lax.ppermute(a, AXES, pairs)


def column_strips():
    return [(m, j) for m, r in enumerate(CHUNKS) for j in range(0, r // 2, 128)]


def plan(k):
    out, at = [], 0
    for strip, (m, _) in enumerate(column_strips()):
        if m <= k:
            out.append((sum(CHUNKS[:k]), CHUNKS[k], strip, at))
            at += CHUNKS[k]
        if m == k and k:
            rows = sum(CHUNKS[:k])
            out.append((0, rows, strip, at))
            at += rows
    return out, at


def half_kernel(rows_ref, cols_ref, count_ref, place_ref, blocks_ref, occ_ref, *refs):
    outs, (acc, turn) = refs[: len(CHUNKS)], refs[len(CHUNKS):]
    step = pl.program_id(0)
    per, naux, wide = blocks_ref.shape
    tiles = wide // 128

    @pl.when(step == 0)
    def _():
        acc[...] = jnp.zeros_like(acc)

    lane = lax.broadcasted_iota(jnp.int32, (W, 128), 1)

    @pl.loop(0, per, unroll=4)
    def _(j):
        s = step * per + j

        col = cols_ref[s]
        pair = occ_ref[:, pl.ds(pl.multiple_of(lax.shift_right_logical(col, 1) * 128, 128), 128)]
        pair = jnp.where(s < count_ref[0], pair.astype(jnp.float32), 0.0)
        other = pltpu.roll(pair, 64, 1)
        odd = (col & 1) == 1
        left = jnp.where(odd, other, pair)
        right = jnp.where(odd, pair, other)
        coeff = jnp.concatenate(
            [jnp.where(lane < 64, left, 0.0), jnp.where(lane < 64, 0.0, right)], axis=0
        ).astype(jnp.bfloat16)
        x = blocks_ref[j].astype(jnp.float32)
        x = jnp.concatenate([x[:, t * 128:(t + 1) * 128] for t in range(tiles)], axis=0)
        prod = lax.dot_general(
            x.astype(jnp.bfloat16), coeff, (((1,), (1,)), ((), ())), preferred_element_type=jnp.float32
        )
        acc[rows_ref[s]] += prod

    @pl.when(step == pl.num_programs(0) - 1)
    def _():
        core = place_ref[0]
        low = lax.broadcasted_iota(jnp.int32, (tiles, 128), 1) < 64
        at = 0
        for k, r in enumerate(CHUNKS):
            span = r // 2 // W
            for h in range(2):
                base = at // W + (h + core - 2 * h * core) * span
                for b in range(span):
                    m = base + b
                    for q in range(naux // 2):
                        even = acc[m, pl.ds(2 * q, tiles, stride=naux), :]
                        odd = acc[m, pl.ds(2 * q + 1, tiles, stride=naux), :]
                        turn[q, pl.ds(0, tiles, stride=2), :] = jnp.where(low, even, pltpu.roll(odd, 64, 1))
                        turn[q, pl.ds(1, tiles, stride=2), :] = jnp.where(low, pltpu.roll(even, 64, 1), odd)
                        outs[k][h, b * W:(b + 1) * W, q * 128:(q + 1) * 128] = turn[q].astype(jnp.bfloat16)
            at += r


def half_rows(blocks, rows, cols, count, place, occ_t):
    slots, naux, wide = blocks.shape
    per = slots // 4
    depth = naux * W
    return pl.pallas_call(
        half_kernel,
        grid_spec=pltpu.PrefetchScalarGridSpec(
            num_scalar_prefetch=4,
            grid=(slots // per,),
            in_specs=[
                pl.BlockSpec((per, naux, wide), lambda i, *_: (i, 0, 0)),
                pl.BlockSpec(occ_t.shape, lambda i, *_: (0, 0)),
            ],
            out_specs=[pl.BlockSpec((2, r // 2, depth), lambda i, *_: (0, 0, 0)) for r in CHUNKS],
            scratch_shapes=[
                pltpu.VMEM((8, naux * wide // 128, 128), jnp.float32),
                pltpu.VMEM((naux // 2, W, 128), jnp.float32),
            ],
        ),
        out_shape=[jax.ShapeDtypeStruct((2, r // 2, depth), jnp.bfloat16) for r in CHUNKS],
        compiler_params=pltpu.CompilerParams(vmem_limit_bytes=56 * MIB),
        cost_estimate=pl.CostEstimate(flops=2 * 10**9, bytes_accessed=8 * 10**6, transcendentals=0),
        name="half_rows",
    )(rows, cols, count, place, blocks, occ_t)


def product_kernel(k, place_ref, *refs):
    n = k + 1
    i_refs, j_refs = refs[:5 * n], refs[5 * n:9 * n]
    packed, own, iv, jv, ob, fb, i_sem, j_sem, out_sem, own_sem = refs[9 * n:]
    core, y, x, z = place_ref[0], place_ref[1], place_ref[2], place_ref[3]
    depth = i_refs[0].shape[-1]
    o, r = sum(CHUNKS[:k]), CHUNKS[k]

    def start(src, where, sem):
        pltpu.make_async_copy(src, where, sem).start()

    at = 0
    for m in range(n):
        half = CHUNKS[m] // 2
        own_j, near_j, near_other_j, far_j = j_refs[4 * m:4 * m + 4]
        for part in range(2):
            for slot, src in enumerate(
                (own_j.at[0, part], near_j.at[0, part], far_j.at[part], near_other_j.at[1 - part])
            ):
                where = jv.at[pl.ds(4 * at + slot * half, half), pl.ds(part * depth, depth)]
                start(src, where, j_sem)
        at += half
    for slot in range(4):
        at = 0
        for m in range(n):
            half = CHUNKS[m] // 2
            own_i, near_i, near_other_i, far_i, far_other_i = i_refs[5 * m:5 * m + 5]
            first = pl.ds(pl.multiple_of(at + core * half, 64), half)
            second = pl.ds(pl.multiple_of(at + (1 - core) * half, 64), half)
            for part in range(2):
                here, there = pl.ds(part * depth, depth), pl.ds((1 - part) * depth, depth)
                sem = i_sem.at[slot]
                if slot == 0:
                    start(own_i.at[0, part], iv.at[slot, first, here], sem)
                    start(own_i.at[1, part], iv.at[slot, second, here], sem)
                elif slot == 1:
                    start(near_i.at[0, part], iv.at[slot, first, here], sem)
                    start(near_i.at[1, part], iv.at[slot, second, here], sem)
                elif slot == 2:
                    start(far_i.at[part], iv.at[slot, first, here], sem)
                    start(far_other_i.at[part], iv.at[slot, second, there], sem)
                else:
                    start(near_other_i.at[0, part], iv.at[slot, second, there], sem)
                    start(near_other_i.at[1, part], iv.at[slot, first, there], sem)
            at += 2 * half
    pltpu.make_async_copy(jv, jv, j_sem).wait()
    pieces, size = plan(k)
    where_strip = column_strips()

    def moved(slot):
        return jnp.where(slot == 0, 0, jnp.where(slot == 2, 2, (slot - 2) * (2 * core - 1)))

    @pl.loop(0, 4)
    def _(slot):
        pltpu.make_async_copy(iv.at[slot], iv.at[slot], i_sem.at[slot]).wait()
        target = (z + moved(slot)) & 3
        nt = (((1,), (1,)), ((), ()))

        def put(result, first_row, first_col):
            for row, rows, strip, at in pieces:
                if row == first_row:
                    m, j = where_strip[strip]
                    for q in range(4):
                        col = 2 * sum(CHUNKS[:m]) + q * (CHUNKS[m] // 2) + j - first_col
                        tile = result[:, col:col + 128]
                        ob[slot, q, at:at + rows, :] = tile.astype(jnp.bfloat16)

                        @pl.when(jnp.logical_and(slot == 0, ((y + moved(q)) & 3) == x))
                        def _():
                            fb[at:at + rows, :] = tile

        put(lax.dot_general(
            iv[slot, o:o + r, :], jv[...], nt, preferred_element_type=jnp.float32
        ), o, 0)
        if o:
            put(lax.dot_general(
                iv[slot, 0:o, :], jv[2 * o:, :], nt, preferred_element_type=jnp.float32
            ), 0, 2 * o)
        for q in range(4):
            to = target * 4 + ((y + moved(q)) & 3)
            start(ob.at[slot, q], packed.at[to], out_sem.at[slot, q])

        @pl.when(slot == 0)
        def _():
            start(fb, own, own_sem)

    pltpu.make_async_copy(fb, own, own_sem).wait()
    for q in range(4):
        for slot in range(4):
            pltpu.make_async_copy(ob.at[slot, q], packed.at[0], out_sem.at[slot, q]).wait()


def product(k, place, i_pieces, j_pieces):
    _, size = plan(k)
    upto = sum(CHUNKS[:k + 1])
    depth = i_pieces[0].shape[-1]
    return pl.pallas_call(
        lambda *refs: product_kernel(k, *refs),
        grid_spec=pltpu.PrefetchScalarGridSpec(
            num_scalar_prefetch=1,
            grid=(1,),
            in_specs=[pl.BlockSpec(memory_space=pl.ANY)] * (len(i_pieces) + len(j_pieces)),
            out_specs=[pl.BlockSpec(memory_space=pl.ANY)] * 2,
            scratch_shapes=[
                pltpu.VMEM((4, upto, 2 * depth), jnp.bfloat16),
                pltpu.VMEM((2 * upto, 2 * depth), jnp.bfloat16),
                pltpu.VMEM((4, 4, size, 128), jnp.bfloat16),
                pltpu.VMEM((size, 128), jnp.float32),
                pltpu.SemaphoreType.DMA((4,)),
                pltpu.SemaphoreType.DMA,
                pltpu.SemaphoreType.DMA((4, 4)),
                pltpu.SemaphoreType.DMA,
            ],
        ),
        out_shape=[
            jax.ShapeDtypeStruct((16, size, 128), jnp.bfloat16),
            jax.ShapeDtypeStruct((size, 128), jnp.float32),
        ],
        compiler_params=pltpu.CompilerParams(vmem_limit_bytes=56 * MIB),
        cost_estimate=pl.CostEstimate(
            flops=2 * 16 * size * 128 * 2 * depth, bytes_accessed=24 * upto * depth, transcendentals=0
        ),
        name="product",
    )(place, *i_pieces, *j_pieces)


def aux_kernel(place_ref, scale_ref, parts, own, keep, give):
    core, x, z = place_ref[0], place_ref[2], place_ref[3]
    for out, side in ((keep, core), (give, 1 - core)):
        for n in range(2):
            source = 2 * side + n
            total = jnp.where(source == z, own[...], parts[4 * source + x].astype(jnp.float32))
            for j in range(1, 4):
                total = total + parts[4 * source + ((x + j) & 3)].astype(jnp.float32)
            out[n] = total * scale_ref[0]


def aux_sum(place, scale, parts, own):
    _, size, _ = parts.shape
    steps = 4
    part = size // steps
    shape = jax.ShapeDtypeStruct((2, size, 128), jnp.float32)
    return pl.pallas_call(
        aux_kernel,
        grid_spec=pltpu.PrefetchScalarGridSpec(
            num_scalar_prefetch=2,
            grid=(steps,),
            in_specs=[
                pl.BlockSpec((16, part, 128), lambda i, *_: (0, i, 0)),
                pl.BlockSpec((part, 128), lambda i, *_: (i, 0)),
            ],
            out_specs=[pl.BlockSpec((2, part, 128), lambda i, *_: (0, i, 0))] * 2,
        ),
        out_shape=[shape, shape],
        compiler_params=pltpu.CompilerParams(vmem_limit_bytes=24 * MIB),
        cost_estimate=pl.CostEstimate(flops=parts.size, bytes_accessed=5 * parts.size, transcendentals=0),
        name="aux_sum",
    )(place, scale, parts, own)


def place_kernel(steps, place_ref, *refs):
    pieces, out, sem = refs[:2 * len(steps)], refs[-2], refs[-1]
    core = place_ref[0]
    copies = []
    for i, k in enumerate(steps):
        for src, half in ((pieces[2 * i], core), (pieces[2 * i + 1], 1 - core)):
            for row, rows, strip, at in plan(k)[0]:
                m, j = column_strips()[strip]
                for n in range(2):
                    base = n * 512 + sum(CHUNKS[:m]) + half * (CHUNKS[m] // 2) + j
                    copy = pltpu.make_async_copy(
                        src.at[n, pl.ds(at, rows)],
                        out.at[pl.ds(row, rows), pl.ds(pl.multiple_of(base, 128), 128)],
                        sem.at[len(copies)],
                    )
                    copy.start()
                    copies.append(copy)
    for copy in copies:
        copy.wait()


def assemble(place, steps, pieces, before):
    count = sum(4 * len(plan(k)[0]) for k in steps)
    ins = list(pieces) + ([before] if before is not None else [])
    return pl.pallas_call(
        lambda *refs: place_kernel(steps, *refs),
        grid_spec=pltpu.PrefetchScalarGridSpec(
            num_scalar_prefetch=1,
            grid=(1,),
            in_specs=[pl.BlockSpec(memory_space=pl.ANY)] * len(ins),
            out_specs=pl.BlockSpec(memory_space=pl.ANY),
            scratch_shapes=[pltpu.SemaphoreType.DMA((count,))],
        ),
        out_shape=jax.ShapeDtypeStruct((512, 1024), jnp.float32),
        input_output_aliases={len(ins): 0} if before is not None else {},
        compiler_params=pltpu.CompilerParams(vmem_limit_bytes=16 * MIB),
        name="assemble",
    )(place, *ins)


def along_z(y, z, x, c):
    return (y, z - 1 + 2 * c, x, c)


def along_y(y, z, x, c):
    return (y - 1 + 2 * c, z, x, c)


def other_core(y, z, x, c):
    return (y, z, x, 1 - c)


def body(blocks, row_block_of_slot, column_block_of_slot, block_count, occupied):
    mu, aux = lax.axis_index("mu"), lax.axis_index("aux")
    place = jnp.stack([aux & 1, mu >> 2, aux >> 1, mu & 3]).astype(jnp.int32)
    total_aux = blocks.shape[1] * lax.axis_size("aux") * occupied.shape[1]
    scale = (1.0 / jnp.sqrt(jnp.float32(total_aux))).reshape(1)
    halves = half_rows(blocks, row_block_of_slot, column_block_of_slot, block_count, place, occupied.T)
    i_pieces, j_pieces, done = [], [], []
    groups = [
        [device_index(y, z, x, c) for z in range(4) for x in range(4)] for y in range(4) for c in range(2)
    ]
    for k, h in enumerate(halves):
        sibling = permute(h, other_core)
        h = jnp.stack([h, sibling[::-1]], axis=1)
        z_near, y_near = permute(h, along_z), permute(h, along_y)
        z_far, y_far = permute(z_near[0], along_z), permute(y_near[0], along_y)
        i_pieces += [h, z_near, permute(z_near, other_core), z_far, permute(z_far, other_core)]
        j_pieces += [h, y_near, permute(y_near[1], other_core), y_far]
        ready = lax.optimization_barrier((place, parts))[0] if k else place
        packed, own = product(k, ready, list(i_pieces), list(j_pieces))
        parts = lax.all_to_all(packed, AXES, 0, 0, tiled=True, axis_index_groups=groups)
        keep, give = aux_sum(place, scale, parts, own)
        done += [keep, permute(give, other_core)]
    last = len(CHUNKS) - 1
    out = assemble(place, range(last), done[:2 * last], None) if last else None
    return assemble(place, [last], done[2 * last:], out)


def solution(mesh):
    return jax.shard_map(
        body,
        mesh=mesh,
        in_specs=(P("mu", "aux", None), P("mu"), P("mu"), P("mu"), P()),
        out_specs=P("mu", "aux"),
        check_vma=False,
    )
```

time: 356 us -> 169 us (0.47)
  waiting for transfers between devices: 249 us -> 56.6 us
  matrix products: 63.5 us -> 0 us
  blocking collectives: 0 us -> 55.3 us
  Pallas kernels: 0 us -> 35.5 us
  local copies, waits for them, and re-layouts: 25.6 us -> 3.94 us
  starting transfers between devices: 0.04 us -> 15.8 us
  between operations: 14.1 us -> 0.79 us
    all_gather x1 -> x0, waiting for transfers between devices: 158 us -> none  [body(): lax.all_gather(local, 'mu', axis=0, tiled=True)]
    reduce_scatter x1 -> x0, waiting for transfers between devices: 90.9 us -> none  [body(): lax.psum_scatter(partial_rows, 'aux', scatter_dimension=1, tiled=True)]
    dot_general x3 -> x0, matrix products: 63.5 us -> none  [the longest x1 29.9 us: body(): jnp.einsum('ms,spai->mapi', onehot, prods, precision=lax.Precision.HIGHEST)]
    ppermute x0 -> x9, waiting for transfers between devices: none -> 56.6 us  [permute(): return lax.ppermute(a, AXES, pairs)]
    all_to_all x0 -> x1, blocking collectives: none -> 55.3 us  [body(): lax.all_to_all(packed, AXES, 0, 0, tiled=True, axis_index_groups=groups)]
    pallas_call x0 -> x4, Pallas kernels: none -> 35.5 us  [the longest x1 22.6 us: product(): pl.pallas_call(lambda *refs: product_kernel(k, *refs), grid_spec=pltpu.Pr...]
    reshape x2 -> x0, local copies, waits for them, and re-layouts: 20 us -> none  [the longest x1 17.9 us: body(): blocks.reshape(number_of_slots, aux_per_shard, BLOCK_WIDTH, BLOCK_WIDTH)]
    ppermute x0 -> x9, starting transfers between devices: none -> 15.8 us  [permute(): return lax.ppermute(a, AXES, pairs)]
  transfers between devices with their start and end apart: 2 -> 9, of which waited for: 2 -> 5; matrix products, arithmetic and copies ran while one was open for 0% -> 0% of each run, Pallas kernels for 0% -> 0%
where the time goes in v2:
time: 169 us
  waiting for transfers between devices  56.6 us (33%)
  blocking collectives  55.3 us (33%)
  Pallas kernels  35.5 us (21%)
  starting transfers between devices  15.8 us (9%)
  local copies, waits for them, and re-layouts  3.94 us (2%)
    ppermute x9, waiting for transfers between devices, permute(): return lax.ppermute(a, AXES, pairs)  56.6 us
    all_to_all x1, blocking collectives, body(): lax.all_to_all(packed, AXES, 0, 0, tiled=True, axis_index_groups=groups)  55.3 us
    pallas_call x1, Pallas kernels, product(): pl.pallas_call(lambda *refs: product_kernel(k, *refs), grid_spec=pltpu.Pr...  22.6 us
    ppermute x9, starting transfers between devices, permute(): return lax.ppermute(a, AXES, pairs)  15.8 us
    pallas_call x1, Pallas kernels, half_rows(): pl.pallas_call(half_kernel, grid_spec=pltpu.PrefetchScalarGridSpec(num_sc...  9.34 us
    unnamed x20, local copies, waits for them, and re-layouts  3.53 us
  transfers between devices with their start and end apart: 9, of which 5 were waited for; matrix products, arithmetic and copies ran while one was open for 0% of the time, Pallas kernels for 0%

profile of v2, /device:TPU:1, one launch (start us, length us, event | category | flops | bytes accessed | tf_op | source)
XLA Modules:
  0.0 168.9 jit_solution(8908275566061497331)
XLA Ops:
  0.7 0.6 pad_add_fusion.place_ref.refs_0_
  1.3 9.3 %half_rows.1 = bf16[2,256,1536]{2,1,0:T(8,128)(2,1)} custom-call(s32[32]{0:T(128)} %rows_ref.1, s32[32]{0:T(128)} %cols_ref.1, s32[1]{0:T(128)S(6)} %copy.6.count_ref, s32[4]{0:T(128)} %pad_add_fusion.place_ref.refs_0_, bf16[32,24,4096]{2,1,0:T(8,128)(2,1)} %blocks_ref.1, bf16[64,8192]{1,0:T(8,128)(2,1)} %bitcast.15), custom_call_target="tpu_custom_call" | custom-call | flops 2000000000 | bytes 8000000 | tf_op jit(solution)/shard_map/half_rows/pallas_call | solution.py:102
  10.6 0.0 copy-start.2
  10.6 1.4 collective-permute-start
  12.0 3.2 %collective-permute-done = bf16[2,256,1536]{2,1,0:T(8,128)(2,1)S(1)} collective-permute-done((bf16[2,256,1536]{2,1,0:T(8,128)(2,1)}, bf16[2,256,1536]{2,1,0:T(8,128)(2,1)S(1)}, u32[]{:S(2)}, u32[]{:S(2)}) %collective-permute-start) | collective-permute-done | bytes 1572896 | tf_op jit(solution)/shard_map/ppermute | solution.py:25
  15.3 0.1 reverse_bitcast_fusion
  15.4 0.0 copy-done.2
  15.4 0.3 pad_maximum_fusion.refs_1_.refs_6_
  15.7 0.0 copy-start.3
  15.7 1.8 %collective-permute-start.1 = (bf16[2,2,256,1536]{3,2,1,0:T(8,128)(2,1)S(1)}, bf16[2,2,256,1536]{3,2,1,0:T(8,128)(2,1)S(1)}, u32[]{:S(2)}, u32[]{:S(2)}) collective-permute-start(bf16[2,2,256,1536]{3,2,1,0:T(8,128)(2,1)S(1)} %pad_maximum_fusion.refs_1_.refs_6_), channel_id=1, source_target_pairs={{0,24},{1,9},{2,26},{3,11},{4,28},{5,13},{6,30},{7,15},{8,0},{9,17... | collective-permute-start | bytes 9437192 | tf_op jit(solution)/shard_map/ppermute | solution.py:25
  17.5 1.3 collective-permute-start.5
  18.8 35.5 %collective-permute-done.1.refs_2_ = bf16[2,2,256,1536]{3,2,1,0:T(8,128)(2,1)S(1)} collective-permute-done((bf16[2,2,256,1536]{3,2,1,0:T(8,128)(2,1)S(1)}, bf16[2,2,256,1536]{3,2,1,0:T(8,128)(2,1)S(1)}, u32[]{:S(2)}, u32[]{:S(2)}) %collective-permute-start.1) | collective-permute-done | bytes 3145760 | tf_op jit(solution)/shard_map/ppermute | solution.py:25
  54.3 0.0 copy-start.5
  54.3 0.1 slice_bitcast_fusion.2
  54.4 0.0 copy-done.3
  54.4 0.1 collective-permute-start.3
  54.5 4.5 %collective-permute-start.2 = (bf16[2,2,256,1536]{3,2,1,0:T(8,128)(2,1)S(1)}, bf16[2,2,256,1536]{3,2,1,0:T(8,128)(2,1)}, u32[]{:S(2)}, u32[]{:S(2)}) collective-permute-start(bf16[2,2,256,1536]{3,2,1,0:T(8,128)(2,1)S(1)} %collective-permute-done.1.refs_2_), channel_id=1, source_target_pairs={{0,1},{1,0},{2,3},{3,2},{4,5},{5,4},{6,7},{7,6},{8,9},{9,8},{10,11... | collective-permute-start | bytes 9437192 | tf_op jit(solution)/shard_map/ppermute | solution.py:25
  58.9 0.0 collective-permute-done.5.refs_7_
  58.9 0.0 copy-start.4
  58.9 0.2 slice_bitcast_fusion
  59.1 0.0 copy-done.5
  59.2 1.4 copy-done.4
  60.6 1.3 collective-permute-start.7
  61.9 1.7 %collective-permute-start.6 = (bf16[2,256,1536]{2,1,0:T(8,128)(2,1)S(1)}, bf16[2,256,1536]{2,1,0:T(8,128)(2,1)S(1)}, u32[]{:S(2)}, u32[]{:S(2)}) collective-permute-start(bf16[2,256,1536]{2,1,0:T(8,128)(2,1)S(1)} %get-tuple-element.14), channel_id=1, source_target_pairs={{0,1},{1,0},{2,3},{3,2},{4,5},{5,4},{6,7},{7,6},{8,9},{9,8},{10,11... | collective-permute-start | bytes 4718600 | tf_op jit(solution)/shard_map/ppermute | solution.py:25
  63.6 11.3 %collective-permute-done.3.refs_4_ = bf16[2,256,1536]{2,1,0:T(8,128)(2,1)S(1)} collective-permute-done((bf16[2,256,1536]{2,1,0:T(8,128)(2,1)S(1)}, bf16[2,256,1536]{2,1,0:T(8,128)(2,1)S(1)}, u32[]{:S(2)}, u32[]{:S(2)}) %collective-permute-start.3) | collective-permute-done | bytes 1572896 | tf_op jit(solution)/shard_map/ppermute | solution.py:25
  74.9 0.0 copy-start.6
  74.9 1.9 %collective-permute-start.4 = (bf16[2,256,1536]{2,1,0:T(8,128)(2,1)S(1)}, bf16[2,256,1536]{2,1,0:T(8,128)(2,1)S(1)}, u32[]{:S(2)}, u32[]{:S(2)}) collective-permute-start(bf16[2,256,1536]{2,1,0:T(8,128)(2,1)S(1)} %collective-permute-done.3.refs_4_), channel_id=1, source_target_pairs={{0,1},{1,0},{2,3},{3,2},{4,5},{5,4},{6,7},{7,6},{8,9},{9,8},{10,11... | collective-permute-start | bytes 4718600 | tf_op jit(solution)/shard_map/ppermute | solution.py:25
  76.9 4.2 %collective-permute-done.7.refs_9_ = bf16[2,256,1536]{2,1,0:T(8,128)(2,1)S(1)} collective-permute-done((bf16[2,256,1536]{2,1,0:T(8,128)(2,1)S(1)}, bf16[2,256,1536]{2,1,0:T(8,128)(2,1)S(1)}, u32[]{:S(2)}, u32[]{:S(2)}) %collective-permute-start.7) | collective-permute-done | bytes 1572896 | tf_op jit(solution)/shard_map/ppermute | solution.py:25
  81.1 0.0 copy-start.7
  81.1 0.0 collective-permute-done.6.refs_8_
  81.1 0.0 copy-start.8
  81.1 0.0 collective-permute-done.4.refs_5_
  81.1 0.0 copy-start.9
  81.1 0.0 collective-permute-done.2.refs_3_
  81.1 0.0 copy-done.6
  81.2 1.1 copy-done.7
  82.3 0.5 copy-done.8
  82.8 0.5 copy-done.9
  83.2 22.6 %product.1 = (bf16[16,1024,128]{2,1,0:T(8,128)(2,1)}, f32[1024,128]{1,0:T(8,128)}) custom-call(s32[4]{0:T(128)} %pad_add_fusion.place_ref.refs_0_, bf16[2,2,256,1536]{3,2,1,0:T(8,128)(2,1)} %copy-done.3, bf16[2,2,256,1536]{3,2,1,0:T(8,128)(2,1)} %copy-done.5, bf16[2,2,256,1536]{3,2,1,0:T(8,128)(2,1)} %collective-permute-done.2.refs_3_, ...), custom_call_target="tpu_custom_call" | custom-call | flops 12884901888 | bytes 18874368 | tf_op jit(solution)/shard_map/product/pallas_call | solution.py:220
  105.8 0.0 copy-start
  105.8 0.0 copy-start.1
  105.9 55.3 %all_to_all.5.parts = bf16[16,1024,128]{2,1,0:T(8,128)(2,1)S(1)} all-to-all(bf16[16,1024,128]{2,1,0:T(8,128)(2,1)} %get-tuple-element.9), channel_id=1, replica_groups={{0,2,4,6,8,10,12,14,16,18,20,22,24,26,28,30},{1,3,5,7,9,11,13,15,17,19,..., dimensions={0} | all-to-all | bytes 8388608 | tf_op jit(solution)/shard_map/all_to_all | solution.py:355
  161.2 0.0 copy-done
  161.2 0.0 copy-done.1
  161.2 1.7 aux_sum.1
  162.9 1.8 %collective-permute-start.8 = (f32[2,1024,128]{2,1,0:T(8,128)S(1)}, f32[2,1024,128]{2,1,0:T(8,128)S(1)}, u32[]{:S(2)}, u32[]{:S(2)}) collective-permute-start(f32[2,1024,128]{2,1,0:T(8,128)S(1)} %get-tuple-element.12), channel_id=1, source_target_pairs={{0,1},{1,0},{2,3},{3,2},{4,5},{5,4},{6,7},{7,6},{8,9},{9,8},{10,11... | collective-permute-start | bytes 3145736 | tf_op jit(solution)/shard_map/ppermute | solution.py:25
  164.7 2.3 %collective-permute-done.8.refs_2_ = f32[2,1024,128]{2,1,0:T(8,128)S(1)} collective-permute-done((f32[2,1024,128]{2,1,0:T(8,128)S(1)}, f32[2,1024,128]{2,1,0:T(8,128)S(1)}, u32[]{:S(2)}, u32[]{:S(2)}) %collective-permute-start.8) | collective-permute-done | bytes 1048608 | tf_op jit(solution)/shard_map/ppermute | solution.py:25
  167.0 1.9 %assemble.1 = f32[512,1024]{1,0:T(8,128)} custom-call(s32[4]{0:T(128)S(1)} %copy-done.1, f32[2,1024,128]{2,1,0:T(8,128)S(1)} %get-tuple-element.11.refs_1_, f32[2,1024,128]{2,1,0:T(8,128)S(1)} %collective-permute-done.8.refs_2_), custom_call_target="tpu_custom_call" | custom-call | tf_op jit(solution)/shard_map/assemble/pallas_call | solution.py:308
Async XLA Ops:
  10.6 4.8 %copy-start.2 = (bf16[2,256,1536]{2,1,0:T(8,128)(2,1)S(1)}, bf16[2,256,1536]{2,1,0:T(8,128)(2,1)}, u32[]{:S(2)}) copy-start(bf16[2,256,1536]{2,1,0:T(8,128)(2,1)} %half_rows.1) | copy-start | bytes 4718596
  10.6 4.7 %collective-permute-start = (bf16[2,256,1536]{2,1,0:T(8,128)(2,1)}, bf16[2,256,1536]{2,1,0:T(8,128)(2,1)S(1)}, u32[]{:S(2)}, u32[]{:S(2)}) collective-permute-start(bf16[2,256,1536]{2,1,0:T(8,128)(2,1)} %half_rows.1), channel_id=1, source_target_pairs={{0,1},{1,0},{2,3},{3,2},{4,5},{5,4},{6,7},{7,6},{8,9},{9,8},{10,11... | collective-permute-start | bytes 4718600 | tf_op jit(solution)/shard_map/ppermute | solution.py:25
  15.7 38.7 %copy-start.3 = (bf16[2,2,256,1536]{3,2,1,0:T(8,128)(2,1)}, bf16[2,2,256,1536]{3,2,1,0:T(8,128)(2,1)S(1)}, u32[]{:S(2)}) copy-start(bf16[2,2,256,1536]{3,2,1,0:T(8,128)(2,1)S(1)} %pad_maximum_fusion.refs_1_.refs_6_) | copy-start | bytes 9437188
  15.7 38.6 %collective-permute-start.1 = (bf16[2,2,256,1536]{3,2,1,0:T(8,128)(2,1)S(1)}, bf16[2,2,256,1536]{3,2,1,0:T(8,128)(2,1)S(1)}, u32[]{:S(2)}, u32[]{:S(2)}) collective-permute-start(bf16[2,2,256,1536]{3,2,1,0:T(8,128)(2,1)S(1)} %pad_maximum_fusion.refs_1_.refs_6_), channel_id=1, source_target_pairs={{0,24},{1,9},{2,26},{3,11},{4,28},{5,13},{6,30},{7,15},{8,0},{9,17... | collective-permute-start | bytes 9437192 | tf_op jit(solution)/shard_map/ppermute | solution.py:25
  17.5 41.4 %collective-permute-start.5 = (bf16[2,2,256,1536]{3,2,1,0:T(8,128)(2,1)S(1)}, bf16[2,2,256,1536]{3,2,1,0:T(8,128)(2,1)S(1)}, u32[]{:S(2)}, u32[]{:S(2)}) collective-permute-start(bf16[2,2,256,1536]{3,2,1,0:T(8,128)(2,1)S(1)} %pad_maximum_fusion.refs_1_.refs_6_), channel_id=1, source_target_pairs={{0,96},{1,33},{2,98},{3,35},{4,100},{5,37},{6,102},{7,39},{8,104},... | collective-permute-start | bytes 9437192 | tf_op jit(solution)/shard_map/ppermute | solution.py:25
  54.3 4.9 %copy-start.5 = (bf16[2,2,256,1536]{3,2,1,0:T(8,128)(2,1)}, bf16[2,2,256,1536]{3,2,1,0:T(8,128)(2,1)S(1)}, u32[]{:S(2)}) copy-start(bf16[2,2,256,1536]{3,2,1,0:T(8,128)(2,1)S(1)} %collective-permute-done.1.refs_2_) | copy-start | bytes 9437188
  54.4 20.5 %collective-permute-start.3 = (bf16[2,256,1536]{2,1,0:T(8,128)(2,1)S(1)}, bf16[2,256,1536]{2,1,0:T(8,128)(2,1)S(1)}, u32[]{:S(2)}, u32[]{:S(2)}) collective-permute-start(bf16[2,256,1536]{2,1,0:T(8,128)(2,1)S(1)} %slice_bitcast_fusion.2), channel_id=1, source_target_pairs={{0,24},{1,9},{2,26},{3,11},{4,28},{5,13},{6,30},{7,15},{8,0},{9,17... | collective-permute-start | bytes 4718600 | tf_op jit(solution)/shard_map/ppermute | solution.py:25
  54.5 26.7 %collective-permute-start.2 = (bf16[2,2,256,1536]{3,2,1,0:T(8,128)(2,1)S(1)}, bf16[2,2,256,1536]{3,2,1,0:T(8,128)(2,1)}, u32[]{:S(2)}, u32[]{:S(2)}) collective-permute-start(bf16[2,2,256,1536]{3,2,1,0:T(8,128)(2,1)S(1)} %collective-permute-done.1.refs_2_), channel_id=1, source_target_pairs={{0,1},{1,0},{2,3},{3,2},{4,5},{5,4},{6,7},{7,6},{8,9},{9,8},{10,11... | collective-permute-start | bytes 9437192 | tf_op jit(solution)/shard_map/ppermute | solution.py:25
  58.9 1.6 copy-start.4
  60.6 20.5 %collective-permute-start.7 = (bf16[2,256,1536]{2,1,0:T(8,128)(2,1)S(1)}, bf16[2,256,1536]{2,1,0:T(8,128)(2,1)S(1)}, u32[]{:S(2)}, u32[]{:S(2)}) collective-permute-start(bf16[2,256,1536]{2,1,0:T(8,128)(2,1)S(1)} %get-tuple-element.13), channel_id=1, source_target_pairs={{0,96},{1,33},{2,98},{3,35},{4,100},{5,37},{6,102},{7,39},{8,104},... | collective-permute-start | bytes 4718600 | tf_op jit(solution)/shard_map/ppermute | solution.py:25
  61.9 19.2 %collective-permute-start.6 = (bf16[2,256,1536]{2,1,0:T(8,128)(2,1)S(1)}, bf16[2,256,1536]{2,1,0:T(8,128)(2,1)S(1)}, u32[]{:S(2)}, u32[]{:S(2)}) collective-permute-start(bf16[2,256,1536]{2,1,0:T(8,128)(2,1)S(1)} %get-tuple-element.14), channel_id=1, source_target_pairs={{0,1},{1,0},{2,3},{3,2},{4,5},{5,4},{6,7},{7,6},{8,9},{9,8},{10,11... | collective-permute-start | bytes 4718600 | tf_op jit(solution)/shard_map/ppermute | solution.py:25
  74.9 6.2 %copy-start.6 = (bf16[2,256,1536]{2,1,0:T(8,128)(2,1)}, bf16[2,256,1536]{2,1,0:T(8,128)(2,1)S(1)}, u32[]{:S(2)}) copy-start(bf16[2,256,1536]{2,1,0:T(8,128)(2,1)S(1)} %collective-permute-done.3.refs_4_) | copy-start | bytes 4718596
  74.9 6.2 %collective-permute-start.4 = (bf16[2,256,1536]{2,1,0:T(8,128)(2,1)S(1)}, bf16[2,256,1536]{2,1,0:T(8,128)(2,1)S(1)}, u32[]{:S(2)}, u32[]{:S(2)}) collective-permute-start(bf16[2,256,1536]{2,1,0:T(8,128)(2,1)S(1)} %collective-permute-done.3.refs_4_), channel_id=1, source_target_pairs={{0,1},{1,0},{2,3},{3,2},{4,5},{5,4},{6,7},{7,6},{8,9},{9,8},{10,11... | collective-permute-start | bytes 4718600 | tf_op jit(solution)/shard_map/ppermute | solution.py:25
  81.1 1.2 copy-start.7
  81.1 1.6 copy-start.8
  81.1 2.1 %copy-start.9 = (bf16[2,256,1536]{2,1,0:T(8,128)(2,1)}, bf16[2,256,1536]{2,1,0:T(8,128)(2,1)S(1)}, u32[]{:S(2)}) copy-start(bf16[2,256,1536]{2,1,0:T(8,128)(2,1)S(1)} %collective-permute-done.4.refs_5_) | copy-start | bytes 4718596
  105.8 55.3 %copy-start = (f32[1024,128]{1,0:T(8,128)S(1)}, f32[1024,128]{1,0:T(8,128)}, u32[]{:S(2)}) copy-start(f32[1024,128]{1,0:T(8,128)} %get-tuple-element.10.own) | copy-start | bytes 1572868
  105.8 55.3 %copy-start.1 = (s32[4]{0:T(128)S(1)}, s32[4]{0:T(128)}, u32[]{:S(2)}) copy-start(s32[4]{0:T(128)} %pad_add_fusion.place_ref.refs_0_) | copy-start | bytes 52
  162.9 4.1 %collective-permute-start.8 = (f32[2,1024,128]{2,1,0:T(8,128)S(1)}, f32[2,1024,128]{2,1,0:T(8,128)S(1)}, u32[]{:S(2)}, u32[]{:S(2)}) collective-permute-start(f32[2,1024,128]{2,1,0:T(8,128)S(1)} %get-tuple-element.12), channel_id=1, source_target_pairs={{0,1},{1,0},{2,3},{3,2},{4,5},{5,4},{6,7},{7,6},{8,9},{9,8},{10,11... | collective-permute-start | bytes 3145736 | tf_op jit(solution)/shard_map/ppermute | solution.py:25

commit v3 on v0

v3 whole, which is shorter than its diff:
```python
import jax
import jax.numpy as jnp
from jax import lax
from jax.experimental import pallas as pl
from jax.experimental.pallas import tpu as pltpu
from jax.sharding import PartitionSpec as P

W = 64
ROWS = 512
HALF = ROWS // 2
AXES = ("mu", "aux")
MIB = 1024 * 1024


def device_index(y, z, x, c):
    return ((y % 4) * 4 + z % 4) * 8 + (x % 4) * 2 + c % 2


def permute(a, move):
    pairs = []
    for y in range(4):
        for z in range(4):
            for x in range(4):
                for c in range(2):
                    pairs.append((device_index(y, z, x, c), device_index(*move(y, z, x, c))))
    return lax.ppermute(a, AXES, pairs)


def half_kernel(rows_ref, cols_ref, count_ref, blocks_ref, occ_ref, out, acc, turn):
    step = pl.program_id(0)
    per, naux, wide = blocks_ref.shape
    tiles = wide // 128

    @pl.when(step == 0)
    def _():
        acc[...] = jnp.zeros_like(acc)

    lane = lax.broadcasted_iota(jnp.int32, (W, 128), 1)

    @pl.loop(0, per, unroll=8)
    def _(j):
        s = step * per + j

        col = cols_ref[s]
        pair = occ_ref[:, pl.ds(pl.multiple_of(lax.shift_right_logical(col, 1) * 128, 128), 128)]
        pair = jnp.where(s < count_ref[0], pair.astype(jnp.float32), 0.0)
        other = pltpu.roll(pair, 64, 1)
        odd = (col & 1) == 1
        left = jnp.where(odd, other, pair)
        right = jnp.where(odd, pair, other)
        coeff = jnp.concatenate(
            [jnp.where(lane < 64, left, 0.0), jnp.where(lane < 64, 0.0, right)], axis=0
        ).astype(jnp.bfloat16)
        x = blocks_ref[j].astype(jnp.float32)
        x = jnp.concatenate([x[:, t * 128:(t + 1) * 128] for t in range(tiles)], axis=0)
        prod = lax.dot_general(
            x.astype(jnp.bfloat16), coeff, (((1,), (1,)), ((), ())), preferred_element_type=jnp.float32
        )
        acc[rows_ref[s]] += prod

    @pl.when(step == pl.num_programs(0) - 1)
    def _():
        core = lax.axis_index("aux") & 1
        low = lax.broadcasted_iota(jnp.int32, (tiles, 128), 1) < 64
        span = HALF // W
        for h in range(2):
            base = (h + core - 2 * h * core) * span
            for b in range(span):
                m = base + b
                for q in range(naux // 2):
                    even = acc[m, pl.ds(2 * q, tiles, stride=naux), :]
                    odd = acc[m, pl.ds(2 * q + 1, tiles, stride=naux), :]
                    turn[q, pl.ds(0, tiles, stride=2), :] = jnp.where(low, even, pltpu.roll(odd, 64, 1))
                    turn[q, pl.ds(1, tiles, stride=2), :] = jnp.where(low, pltpu.roll(even, 64, 1), odd)
                    out[h, b * W:(b + 1) * W, q * 128:(q + 1) * 128] = turn[q].astype(jnp.bfloat16)


def half_rows(blocks, rows, cols, count, occ_t):
    slots, naux, wide = blocks.shape
    per = slots // 4
    depth = naux * W
    return pl.pallas_call(
        half_kernel,
        grid_spec=pltpu.PrefetchScalarGridSpec(
            num_scalar_prefetch=3,
            grid=(slots // per,),
            in_specs=[
                pl.BlockSpec((per, naux, wide), lambda i, *_: (i, 0, 0)),
                pl.BlockSpec(occ_t.shape, lambda i, *_: (0, 0)),
            ],
            out_specs=pl.BlockSpec((2, HALF, depth), lambda i, *_: (0, 0, 0)),
            scratch_shapes=[
                pltpu.VMEM((8, naux * wide // 128, 128), jnp.float32),
                pltpu.VMEM((naux // 2, W, 128), jnp.float32),
            ],
        ),
        out_shape=jax.ShapeDtypeStruct((2, HALF, depth), jnp.bfloat16),
        compiler_params=pltpu.CompilerParams(vmem_limit_bytes=56 * MIB),
        cost_estimate=pl.CostEstimate(flops=2 * 10**9, bytes_accessed=8 * 10**6, transcendentals=0),
        name="half_rows",
    )(rows, cols, count, blocks, occ_t)


STRIPS = HALF // 128


def moved(slot, core):
    return jnp.where(slot == 0, 0, jnp.where(slot == 3, 2, (2 * slot - 3) * (2 * core - 1)))


def product_kernel(late, place_ref, *refs):
    units, slots = (8, 4) if late else (5, 3)
    rows, refs = refs[:units], refs[units:]
    columns, refs = refs[:slots], refs[slots:]
    packed, iv, jv, ob, i_sem, j_sem, out_sem = refs[1 if late else 0:]
    core, y, z = place_ref[0], place_ref[1], place_ref[3]
    depth = rows[0].shape[-1]
    lanes = (pl.ds(0, depth), pl.ds(depth, depth))

    def start(src, where, sem):
        pltpu.make_async_copy(src, where, sem).start()

    def load_rows(unit):
        for p in range(2):
            start(rows[unit].at[p], iv.at[unit, :, lanes[1 - p if unit in (3, 5, 7) else p]], i_sem.at[unit])

    def load_columns(q):
        for p in range(2):
            start(columns[q].at[p], jv.at[pl.ds(q * HALF, HALF), lanes[1 - p if q == 2 else p]], j_sem)

    def wait_rows(unit):
        pltpu.make_async_copy(iv.at[unit], iv.at[unit], i_sem.at[unit]).wait()

    def multiply(unit, first, last):
        result = lax.dot_general(
            iv[unit], jv[first * HALF:last * HALF, :], (((1,), (1,)), ((), ())), preferred_element_type=jnp.float32
        )
        slot = jnp.where(unit < 2, 0, jnp.where(unit >= 6, 3, jnp.where(unit % 2 == 1, 2, 1)))
        mine = jnp.logical_or(unit == 0, jnp.logical_or(unit == 2, jnp.logical_or(unit == 5, unit == 6)))
        span = pl.ds(pl.multiple_of(jnp.where(mine, core, 1 - core) * HALF, HALF), HALF)
        row = ((z + moved(slot, core)) & 3) * 4
        for q in range(first, last):
            for j in range(STRIPS):
                col = (q - first) * HALF + j * 128
                ob[unit, q, j] = result[:, col:col + 128].astype(jnp.bfloat16)
            to = row + ((y + moved(q, core)) & 3)
            start(ob.at[unit, q], packed.at[to, :, span], out_sem.at[unit])

    def finish(unit, first, last):
        whole = ob.at[unit, pl.ds(first, last - first)]
        pltpu.make_async_copy(whole, whole, out_sem.at[unit]).wait()

    for q in range(slots):
        load_columns(q)
    if late:
        for unit in (5, 6, 7, 0, 1, 2, 3, 4):
            load_rows(unit)
    else:
        for unit in range(5):
            load_rows(unit)
    pltpu.make_async_copy(jv, jv, j_sem).wait()

    if late:
        @pl.loop(5, 8)
        def _(unit):
            wait_rows(unit)
            multiply(unit, 0, 4)

    @pl.loop(0, 5)
    def _(unit):
        wait_rows(unit)
        multiply(unit, *((3, 4) if late else (0, 3)))

    if late:
        @pl.loop(5, 8)
        def _(unit):
            finish(unit, 0, 4)

    @pl.loop(0, 5)
    def _(unit):
        finish(unit, *((3, 4) if late else (0, 3)))


def product(late, place, rows, columns, before=()):
    depth = rows[0].shape[-1]
    ins = list(rows) + list(columns) + list(before)
    units, slots = len(rows), len(columns)
    return pl.pallas_call(
        lambda *refs: product_kernel(late, *refs),
        grid_spec=pltpu.PrefetchScalarGridSpec(
            num_scalar_prefetch=1,
            grid=(1,),
            in_specs=[pl.BlockSpec(memory_space=pl.ANY)] * len(ins),
            out_specs=pl.BlockSpec(memory_space=pl.ANY),
            scratch_shapes=[
                pltpu.VMEM((units, HALF, 2 * depth), jnp.bfloat16),
                pltpu.VMEM((slots * HALF, 2 * depth), jnp.bfloat16),
                pltpu.VMEM((units, slots, STRIPS, HALF, 128), jnp.bfloat16),
                pltpu.SemaphoreType.DMA((units,)),
                pltpu.SemaphoreType.DMA,
                pltpu.SemaphoreType.DMA((units,)),
            ],
        ),
        out_shape=jax.ShapeDtypeStruct((16, STRIPS, ROWS, 128), jnp.bfloat16),
        input_output_aliases={len(ins): 0} if late else {},
        compiler_params=pltpu.CompilerParams(vmem_limit_bytes=(30 if late else 20) * MIB),
        cost_estimate=pl.CostEstimate(
            flops=(17 if late else 15) * HALF * HALF * 2 * 2 * depth, bytes_accessed=(units + slots) * ROWS * 2 * depth,
            transcendentals=0,
        ),
        name="product_late" if late else "product_early",
    )(place, *ins)


def sum_kernel(keep, place_ref, scale_ref, parts, out):
    core = place_ref[0]
    for n in range(2):
        total = parts[4 * n].astype(jnp.float32)
        for j in range(1, 4):
            total = total + parts[4 * n + j].astype(jnp.float32)
        total = total * scale_ref[0]
        if keep:
            for j in range(STRIPS):
                base = n * ROWS + core * HALF + j * 128
                out[:, pl.ds(pl.multiple_of(base, 128), 128)] = total[j]
        else:
            out[n] = total


def aux_sum(keep, place, scale, parts):
    steps = 4
    rows = ROWS // steps
    if keep:
        out_spec = pl.BlockSpec((rows, 2 * ROWS), lambda i, *_: (i, 0))
        shape = (ROWS, 2 * ROWS)
    else:
        out_spec = pl.BlockSpec((2, STRIPS, rows, 128), lambda i, *_: (0, 0, i, 0))
        shape = (2, STRIPS, ROWS, 128)
    return pl.pallas_call(
        lambda *refs: sum_kernel(keep, *refs),
        grid_spec=pltpu.PrefetchScalarGridSpec(
            num_scalar_prefetch=2,
            grid=(steps,),
            in_specs=[
                pl.BlockSpec(
                    (8, STRIPS, rows, 128), lambda i, place, _: (place[0] if keep else 1 - place[0], 0, i, 0)
                ),
            ],
            out_specs=out_spec,
        ),
        out_shape=jax.ShapeDtypeStruct(shape, jnp.float32),
        compiler_params=pltpu.CompilerParams(vmem_limit_bytes=24 * MIB),
        cost_estimate=pl.CostEstimate(flops=parts.size, bytes_accessed=3 * parts.size, transcendentals=0),
        name="sum_keep" if keep else "sum_give",
    )(place, scale, parts)


def place_kernel(place_ref, src, before, out, sem):
    core = place_ref[0]
    copies = []
    for n in range(2):
        for j in range(HALF // 128):
            base = n * ROWS + (1 - core) * HALF + j * 128
            copies.append(pltpu.make_async_copy(
                src.at[n, j], out.at[:, pl.ds(pl.multiple_of(base, 128), 128)], sem.at[n, j]
            ))
    for copy in copies:
        copy.start()
    for copy in copies:
        copy.wait()


def assemble(place, received, before):
    return pl.pallas_call(
        place_kernel,
        grid_spec=pltpu.PrefetchScalarGridSpec(
            num_scalar_prefetch=1,
            grid=(1,),
            in_specs=[pl.BlockSpec(memory_space=pl.ANY)] * 2,
            out_specs=pl.BlockSpec(memory_space=pl.ANY),
            scratch_shapes=[pltpu.SemaphoreType.DMA((2, HALF // 128))],
        ),
        out_shape=jax.ShapeDtypeStruct((ROWS, 2 * ROWS), jnp.float32),
        input_output_aliases={2: 0},
        compiler_params=pltpu.CompilerParams(vmem_limit_bytes=16 * MIB),
        name="assemble",
    )(place, received, before)


def along_z(y, z, x, c):
    return (y, z - 1 + 2 * c, x, c)


def along_y(y, z, x, c):
    return (y - 1 + 2 * c, z, x, c)


def across_y(y, z, x, c):
    return (y - 1 + 2 * c, z, x, 1 - c)


def other_core(y, z, x, c):
    return (y, z, x, 1 - c)


def body(blocks, row_block_of_slot, column_block_of_slot, block_count, occupied):
    mu, aux = lax.axis_index("mu"), lax.axis_index("aux")
    place = jnp.stack([aux & 1, mu >> 2, aux >> 1, mu & 3]).astype(jnp.int32)
    total_aux = blocks.shape[1] * lax.axis_size("aux") * occupied.shape[1]
    scale = (1.0 / jnp.sqrt(jnp.float32(total_aux))).reshape(1)
    groups = [
        [device_index(y, z, x, c) for z in range(4) for x in range(4)] for y in range(4) for c in range(2)
    ]
    h = half_rows(blocks, row_block_of_slot, column_block_of_slot, block_count, occupied.T)
    sibling = permute(h, other_core)
    own = [jnp.stack([h[0], sibling[1]]), jnp.stack([h[1], sibling[0]])]
    z_near = [permute(a, along_z) for a in own]
    y_near, y_other = permute(own[0], along_y), permute(own[1], across_y)
    z_far, y_far = permute(z_near[0], along_z), permute(y_near, along_y)
    z_other = [permute(a, other_core) for a in z_near]
    rows, columns = own + [z_near[0], z_other[0], z_near[1]], [own[0], y_near, y_other]
    early = product(False, place, rows, columns)
    z_far, y_far, early = lax.optimization_barrier((z_far, y_far, early))
    rows, columns = rows + [z_other[1], z_far, permute(z_far, other_core)], columns + [y_far]
    packed = product(True, place, rows, columns, [early])
    parts = lax.all_to_all(packed, AXES, 0, 0, tiled=True, axis_index_groups=groups)
    give = aux_sum(False, place, scale, parts)
    received = permute(give, other_core)
    return assemble(place, received, aux_sum(True, place, scale, parts))


def solution(mesh):
    return jax.shard_map(
        body,
        mesh=mesh,
        in_specs=(P("mu", "aux", None), P("mu"), P("mu"), P("mu"), P()),
        out_specs=P("mu", "aux"),
        check_vma=False,
    )
```

time: 356 us -> 152 us (0.43)
  waiting for transfers between devices: 249 us -> 40.2 us
  matrix products: 63.5 us -> 0 us
  blocking collectives: 0 us -> 54.3 us
  Pallas kernels: 0 us -> 38.2 us
  local copies, waits for them, and re-layouts: 25.6 us -> 1.57 us
  starting transfers between devices: 0.04 us -> 16 us
  between operations: 14.1 us -> 0.71 us
  other arithmetic: 3.97 us -> 0.37 us
    all_gather x1 -> x0, waiting for transfers between devices: 158 us -> none  [body(): lax.all_gather(local, 'mu', axis=0, tiled=True)]
    reduce_scatter x1 -> x0, waiting for transfers between devices: 90.9 us -> none  [body(): lax.psum_scatter(partial_rows, 'aux', scatter_dimension=1, tiled=True)]
    dot_general x3 -> x0, matrix products: 63.5 us -> none  [the longest x1 29.9 us: body(): jnp.einsum('ms,spai->mapi', onehot, prods, precision=lax.Precision.HIGHEST)]
    all_to_all x0 -> x1, blocking collectives: none -> 54.3 us  [body(): lax.all_to_all(packed, AXES, 0, 0, tiled=True, axis_index_groups=groups)]
    ppermute x0 -> x11, waiting for transfers between devices: none -> 40.2 us  [permute(): return lax.ppermute(a, AXES, pairs)]
    pallas_call x0 -> x6, Pallas kernels: none -> 38.2 us  [the longest x2 24.3 us: product(): pl.pallas_call(lambda *refs: product_kernel(late, *refs), grid_spec=pltpu...]
    reshape x2 -> x0, local copies, waits for them, and re-layouts: 20 us -> none  [the longest x1 17.9 us: body(): blocks.reshape(number_of_slots, aux_per_shard, BLOCK_WIDTH, BLOCK_WIDTH)]
    ppermute x0 -> x11, starting transfers between devices: none -> 16 us  [permute(): return lax.ppermute(a, AXES, pairs)]
  transfers between devices with their start and end apart: 2 -> 11, of which waited for: 2 -> 6; matrix products, arithmetic and copies ran while one was open for 0% -> 1% of each run, Pallas kernels for 0% -> 9%
where the time goes in v3:
time: 152 us; the launch traced here: 151 us
  blocking collectives  54.3 us (36%)
  waiting for transfers between devices  40.2 us (26%)
  Pallas kernels  38.2 us (25%)
  starting transfers between devices  16 us (11%)
  local copies, waits for them, and re-layouts  1.57 us (1%)
    all_to_all x1, blocking collectives, body(): lax.all_to_all(packed, AXES, 0, 0, tiled=True, axis_index_groups=groups)  54.3 us
    ppermute x11, waiting for transfers between devices, permute(): return lax.ppermute(a, AXES, pairs)  40.2 us
    pallas_call x2, Pallas kernels, product(): pl.pallas_call(lambda *refs: product_kernel(late, *refs), grid_spec=pltpu...  24.3 us
    ppermute x11, starting transfers between devices, permute(): return lax.ppermute(a, AXES, pairs)  16 us
    pallas_call x1, Pallas kernels, half_rows(): pl.pallas_call(half_kernel, grid_spec=pltpu.PrefetchScalarGridSpec(num_sc...  8.63 us
    pallas_call x2, Pallas kernels, aux_sum(): pl.pallas_call(lambda *refs: sum_kernel(keep, *refs), grid_spec=pltpu.Pre...  3.71 us
  transfers between devices with their start and end apart: 11, of which 6 were waited for; matrix products, arithmetic and copies ran while one was open for 1% of the time, Pallas kernels for 9%

profile of v3, /device:TPU:1, one launch (start us, length us, event | category | flops | bytes accessed | tf_op | source)
XLA Modules:
  0.0 151.3 jit_solution(9706104829499812061)
XLA Ops:
  0.7 8.6 %half_rows.1 = bf16[2,256,1536]{2,1,0:T(8,128)(2,1)} custom-call(s32[32]{0:T(128)} %rows_ref.1, s32[32]{0:T(128)} %cols_ref.1, s32[1]{0:T(128)S(6)} %copy.10.count_ref, bf16[32,24,4096]{2,1,0:T(8,128)(2,1)} %blocks_ref.1, bf16[64,8192]{1,0:T(8,128)(2,1)} %bitcast.5), custom_call_target="tpu_custom_call" | custom-call | flops 2000000000 | bytes 8000000 | tf_op jit(solution)/shard_map/half_rows/pallas_call | solution.py:82
  9.3 1.4 collective-permute-start
  10.7 1.5 fusion
  12.2 1.8 %collective-permute-done = bf16[2,256,1536]{2,1,0:T(8,128)(2,1)S(1)} collective-permute-done((bf16[2,256,1536]{2,1,0:T(8,128)(2,1)}, bf16[2,256,1536]{2,1,0:T(8,128)(2,1)S(1)}, u32[]{:S(2)}, u32[]{:S(2)}) %collective-permute-start) | collective-permute-done | bytes 1572896 | tf_op jit(solution)/shard_map/ppermute | solution.py:26
  14.0 0.1 fusion.1
  14.1 0.1 pad_maximum_fusion.refs_1_.refs_6_.refs_9_
  14.2 1.8 %collective-permute-start.1 = (bf16[2,256,1536]{2,1,0:T(8,128)(2,1)S(1)}, bf16[2,256,1536]{2,1,0:T(8,128)(2,1)}, u32[]{:S(2)}, u32[]{:S(2)}) collective-permute-start(bf16[2,256,1536]{2,1,0:T(8,128)(2,1)S(1)} %pad_maximum_fusion.refs_1_.refs_6_.refs_9_), channel_id=1, source_target_pairs={{0,24},{1,9},{2,26},{3,11},{4,28},{5,13},{6,30},{7,15},{8,0},{9,17... | collective-permute-start | bytes 4718600 | tf_op jit(solution)/shard_map/ppermute | solution.py:26
  16.0 1.3 collective-permute-start.6
  17.3 0.1 pad_maximum_fusion.1.refs_2_
  17.4 1.7 %collective-permute-start.3 = (bf16[2,256,1536]{2,1,0:T(8,128)(2,1)S(1)}, bf16[2,256,1536]{2,1,0:T(8,128)(2,1)}, u32[]{:S(2)}, u32[]{:S(2)}) collective-permute-start(bf16[2,256,1536]{2,1,0:T(8,128)(2,1)S(1)} %pad_maximum_fusion.1.refs_2_), channel_id=1, source_target_pairs={{0,24},{1,9},{2,26},{3,11},{4,28},{5,13},{6,30},{7,15},{8,0},{9,17... | collective-permute-start | bytes 4718600 | tf_op jit(solution)/shard_map/ppermute | solution.py:26
  19.2 1.9 %collective-permute-start.8 = (bf16[2,256,1536]{2,1,0:T(8,128)(2,1)S(1)}, bf16[2,256,1536]{2,1,0:T(8,128)(2,1)}, u32[]{:S(2)}, u32[]{:S(2)}) collective-permute-start(bf16[2,256,1536]{2,1,0:T(8,128)(2,1)S(1)} %pad_maximum_fusion.1.refs_2_), channel_id=1, source_target_pairs={{0,97},{1,32},{2,99},{3,34},{4,101},{5,36},{6,103},{7,38},{8,105},... | collective-permute-start | bytes 4718600 | tf_op jit(solution)/shard_map/ppermute | solution.py:26
  21.0 15.0 %collective-permute-done.1.refs_3_ = bf16[2,256,1536]{2,1,0:T(8,128)(2,1)} collective-permute-done((bf16[2,256,1536]{2,1,0:T(8,128)(2,1)S(1)}, bf16[2,256,1536]{2,1,0:T(8,128)(2,1)}, u32[]{:S(2)}, u32[]{:S(2)}) %collective-permute-start.1) | collective-permute-done | bytes 1572896 | tf_op jit(solution)/shard_map/ppermute | solution.py:26
  36.0 0.7 collective-permute-start.2
  36.7 0.0 collective-permute-done.6.refs_7_.refs_10_
  36.7 1.3 collective-permute-start.7
  38.0 0.6 collective-permute-start.5
  38.6 0.1 pad_add_fusion.refs_0_.place_ref
  38.7 14.5 %collective-permute-done.3.refs_5_ = bf16[2,256,1536]{2,1,0:T(8,128)(2,1)} collective-permute-done((bf16[2,256,1536]{2,1,0:T(8,128)(2,1)S(1)}, bf16[2,256,1536]{2,1,0:T(8,128)(2,1)}, u32[]{:S(2)}, u32[]{:S(2)}) %collective-permute-start.3) | collective-permute-done | bytes 1572896 | tf_op jit(solution)/shard_map/ppermute | solution.py:26
  53.2 0.4 collective-permute-start.4
  53.6 2.2 %collective-permute-done.8.refs_8_.refs_11_ = bf16[2,256,1536]{2,1,0:T(8,128)(2,1)} collective-permute-done((bf16[2,256,1536]{2,1,0:T(8,128)(2,1)S(1)}, bf16[2,256,1536]{2,1,0:T(8,128)(2,1)}, u32[]{:S(2)}, u32[]{:S(2)}) %collective-permute-start.8) | collective-permute-done | bytes 1572896 | tf_op jit(solution)/shard_map/ppermute | solution.py:26
  55.8 0.0 collective-permute-done.2.refs_4_
  55.8 11.1 %product_early.1.refs_13_ = bf16[16,2,512,128]{3,2,1,0:T(8,128)(2,1)S(1)} custom-call(s32[4]{0:T(128)S(1)} %pad_add_fusion.refs_0_.place_ref, bf16[2,256,1536]{2,1,0:T(8,128)(2,1)S(1)} %pad_maximum_fusion.refs_1_.refs_6_.refs_9_, bf16[2,256,1536]{2,1,0:T(8,128)(2,1)S(1)} %pad_maximum_fusion.1.refs_2_, bf16[2,256,1536]{2,1,0:T(8,128)(2,1)} %collective-permute-done.1.refs_3_, ...), custom_call_target="tpu_custom_call" | custom-call | flops 6039797760 | bytes 12582912 | tf_op jit(solution)/shard_map/product_early/pallas_call | solution.py:188
  66.9 3.5 %collective-permute-done.7.refs_12_ = bf16[2,256,1536]{2,1,0:T(8,128)(2,1)} collective-permute-done((bf16[2,256,1536]{2,1,0:T(8,128)(2,1)}, bf16[2,256,1536]{2,1,0:T(8,128)(2,1)}, u32[]{:S(2)}, u32[]{:S(2)}) %collective-permute-start.7) | collective-permute-done | bytes 1572896 | tf_op jit(solution)/shard_map/ppermute | solution.py:26
  70.4 0.0 collective-permute-done.5.refs_7_
  70.4 3.2 %collective-permute-start.9 = (bf16[2,256,1536]{2,1,0:T(8,128)(2,1)}, bf16[2,256,1536]{2,1,0:T(8,128)(2,1)S(1)}, u32[]{:S(2)}, u32[]{:S(2)}) collective-permute-start(bf16[2,256,1536]{2,1,0:T(8,128)(2,1)} %collective-permute-done.5.refs_7_), channel_id=1, source_target_pairs={{0,1},{1,0},{2,3},{3,2},{4,5},{5,4},{6,7},{7,6},{8,9},{9,8},{10,11... | collective-permute-start | bytes 4718600 | tf_op jit(solution)/shard_map/ppermute | solution.py:26
  73.5 0.0 collective-permute-done.4.refs_6_
  73.5 3.2 %collective-permute-done.9.refs_8_ = bf16[2,256,1536]{2,1,0:T(8,128)(2,1)S(1)} collective-permute-done((bf16[2,256,1536]{2,1,0:T(8,128)(2,1)}, bf16[2,256,1536]{2,1,0:T(8,128)(2,1)S(1)}, u32[]{:S(2)}, u32[]{:S(2)}) %collective-permute-start.9) | collective-permute-done | bytes 1572896 | tf_op jit(solution)/shard_map/ppermute | solution.py:26
  76.8 13.2 %product_late.1 = bf16[16,2,512,128]{3,2,1,0:T(8,128)(2,1)S(1)} custom-call(s32[4]{0:T(128)S(1)} %pad_add_fusion.refs_0_.place_ref, bf16[2,256,1536]{2,1,0:T(8,128)(2,1)S(1)} %pad_maximum_fusion.refs_1_.refs_6_.refs_9_, bf16[2,256,1536]{2,1,0:T(8,128)(2,1)S(1)} %pad_maximum_fusion.1.refs_2_, ...), custom_call_target="tpu_custom_call", output_to_operand_aliasing={{}: (13, {})} | custom-call | flops 6845104128 | bytes 18874368 | tf_op jit(solution)/shard_map/product_late/pallas_call | solution.py:188
  90.0 54.3 %all_to_all.5.refs_2_ = bf16[16,2,512,128]{3,2,1,0:T(8,128)(2,1)S(1)} all-to-all(bf16[16,2,512,128]{3,2,1,0:T(8,128)(2,1)S(1)} %product_late.1), channel_id=1, replica_groups={{0,2,4,6,8,10,12,14,16,18,20,22,24,26,28,30},{1,3,5,7,9,11,13,15,17,19,..., dimensions={0} | all-to-all | bytes 8388608 | tf_op jit(solution)/shard_map/all_to_all | solution.py:326
  144.3 1.1 sum_give.1
  145.4 1.7 %collective-permute-start.10 = (f32[2,2,512,128]{3,2,1,0:T(8,128)S(1)}, f32[2,2,512,128]{3,2,1,0:T(8,128)S(1)}, u32[]{:S(2)}, u32[]{:S(2)}) collective-permute-start(f32[2,2,512,128]{3,2,1,0:T(8,128)S(1)} %sum_give.1), channel_id=1, source_target_pairs={{0,1},{1,0},{2,3},{3,2},{4,5},{5,4},{6,7},{7,6},{8,9},{9,8},{10,11... | collective-permute-start | bytes 3145736 | tf_op jit(solution)/shard_map/ppermute | solution.py:26
  147.2 2.6 %sum_keep.1.before = f32[512,1024]{1,0:T(8,128)} custom-call(s32[4]{0:T(128)S(1)} %pad_add_fusion.refs_0_.place_ref, f32[1]{0:T(128)} %constant.16.clone.1.refs_1_, bf16[16,2,512,128]{3,2,1,0:T(8,128)(2,1)S(1)} %all_to_all.5.refs_2_), custom_call_target="tpu_custom_call" | custom-call | flops 2097152 | bytes 6291456 | tf_op jit(solution)/shard_map/sum_keep/pallas_call | solution.py:239
  149.8 0.0 collective-permute-done.10.src
  149.8 1.5 %assemble.1 = f32[512,1024]{1,0:T(8,128)} custom-call(s32[4]{0:T(128)S(1)} %pad_add_fusion.refs_0_.place_ref, f32[2,2,512,128]{3,2,1,0:T(8,128)S(1)} %collective-permute-done.10.src, f32[512,1024]{1,0:T(8,128)} %sum_keep.1.before), custom_call_target="tpu_custom_call", output_to_operand_aliasing={{}: (2, {})} | custom-call | tf_op jit(solution)/shard_map/assemble/pallas_call | solution.py:274
Async XLA Ops:
  9.3 4.7 %collective-permute-start = (bf16[2,256,1536]{2,1,0:T(8,128)(2,1)}, bf16[2,256,1536]{2,1,0:T(8,128)(2,1)S(1)}, u32[]{:S(2)}, u32[]{:S(2)}) collective-permute-start(bf16[2,256,1536]{2,1,0:T(8,128)(2,1)} %half_rows.1), channel_id=1, source_target_pairs={{0,1},{1,0},{2,3},{3,2},{4,5},{5,4},{6,7},{7,6},{8,9},{9,8},{10,11... | collective-permute-start | bytes 4718600 | tf_op jit(solution)/shard_map/ppermute | solution.py:26
  14.2 21.8 %collective-permute-start.1 = (bf16[2,256,1536]{2,1,0:T(8,128)(2,1)S(1)}, bf16[2,256,1536]{2,1,0:T(8,128)(2,1)}, u32[]{:S(2)}, u32[]{:S(2)}) collective-permute-start(bf16[2,256,1536]{2,1,0:T(8,128)(2,1)S(1)} %pad_maximum_fusion.refs_1_.refs_6_.refs_9_), channel_id=1, source_target_pairs={{0,24},{1,9},{2,26},{3,11},{4,28},{5,13},{6,30},{7,15},{8,0},{9,17... | collective-permute-start | bytes 4718600 | tf_op jit(solution)/shard_map/ppermute | solution.py:26
  16.0 20.7 %collective-permute-start.6 = (bf16[2,256,1536]{2,1,0:T(8,128)(2,1)S(1)}, bf16[2,256,1536]{2,1,0:T(8,128)(2,1)}, u32[]{:S(2)}, u32[]{:S(2)}) collective-permute-start(bf16[2,256,1536]{2,1,0:T(8,128)(2,1)S(1)} %pad_maximum_fusion.refs_1_.refs_6_.refs_9_), channel_id=1, source_target_pairs={{0,96},{1,33},{2,98},{3,35},{4,100},{5,37},{6,102},{7,39},{8,104},... | collective-permute-start | bytes 4718600 | tf_op jit(solution)/shard_map/ppermute | solution.py:26
  17.4 35.7 %collective-permute-start.3 = (bf16[2,256,1536]{2,1,0:T(8,128)(2,1)S(1)}, bf16[2,256,1536]{2,1,0:T(8,128)(2,1)}, u32[]{:S(2)}, u32[]{:S(2)}) collective-permute-start(bf16[2,256,1536]{2,1,0:T(8,128)(2,1)S(1)} %pad_maximum_fusion.1.refs_2_), channel_id=1, source_target_pairs={{0,24},{1,9},{2,26},{3,11},{4,28},{5,13},{6,30},{7,15},{8,0},{9,17... | collective-permute-start | bytes 4718600 | tf_op jit(solution)/shard_map/ppermute | solution.py:26
  19.2 36.6 %collective-permute-start.8 = (bf16[2,256,1536]{2,1,0:T(8,128)(2,1)S(1)}, bf16[2,256,1536]{2,1,0:T(8,128)(2,1)}, u32[]{:S(2)}, u32[]{:S(2)}) collective-permute-start(bf16[2,256,1536]{2,1,0:T(8,128)(2,1)S(1)} %pad_maximum_fusion.1.refs_2_), channel_id=1, source_target_pairs={{0,97},{1,32},{2,99},{3,34},{4,101},{5,36},{6,103},{7,38},{8,105},... | collective-permute-start | bytes 4718600 | tf_op jit(solution)/shard_map/ppermute | solution.py:26
  36.0 19.7 %collective-permute-start.2 = (bf16[2,256,1536]{2,1,0:T(8,128)(2,1)}, bf16[2,256,1536]{2,1,0:T(8,128)(2,1)}, u32[]{:S(2)}, u32[]{:S(2)}) collective-permute-start(bf16[2,256,1536]{2,1,0:T(8,128)(2,1)} %collective-permute-done.1.refs_3_), channel_id=1, source_target_pairs={{0,1},{1,0},{2,3},{3,2},{4,5},{5,4},{6,7},{7,6},{8,9},{9,8},{10,11... | collective-permute-start | bytes 4718600 | tf_op jit(solution)/shard_map/ppermute | solution.py:26
  36.7 33.6 %collective-permute-start.7 = (bf16[2,256,1536]{2,1,0:T(8,128)(2,1)}, bf16[2,256,1536]{2,1,0:T(8,128)(2,1)}, u32[]{:S(2)}, u32[]{:S(2)}) collective-permute-start(bf16[2,256,1536]{2,1,0:T(8,128)(2,1)} %collective-permute-done.6.refs_7_.refs_10_), channel_id=1, source_target_pairs={{0,96},{1,33},{2,98},{3,35},{4,100},{5,37},{6,102},{7,39},{8,104},... | collective-permute-start | bytes 4718600 | tf_op jit(solution)/shard_map/ppermute | solution.py:26
  38.0 32.3 %collective-permute-start.5 = (bf16[2,256,1536]{2,1,0:T(8,128)(2,1)}, bf16[2,256,1536]{2,1,0:T(8,128)(2,1)}, u32[]{:S(2)}, u32[]{:S(2)}) collective-permute-start(bf16[2,256,1536]{2,1,0:T(8,128)(2,1)} %collective-permute-done.1.refs_3_), channel_id=1, source_target_pairs={{0,24},{1,9},{2,26},{3,11},{4,28},{5,13},{6,30},{7,15},{8,0},{9,17... | collective-permute-start | bytes 4718600 | tf_op jit(solution)/shard_map/ppermute | solution.py:26
  53.2 20.4 %collective-permute-start.4 = (bf16[2,256,1536]{2,1,0:T(8,128)(2,1)}, bf16[2,256,1536]{2,1,0:T(8,128)(2,1)S(1)}, u32[]{:S(2)}, u32[]{:S(2)}) collective-permute-start(bf16[2,256,1536]{2,1,0:T(8,128)(2,1)} %collective-permute-done.3.refs_5_), channel_id=1, source_target_pairs={{0,1},{1,0},{2,3},{3,2},{4,5},{5,4},{6,7},{7,6},{8,9},{9,8},{10,11... | collective-permute-start | bytes 4718600 | tf_op jit(solution)/shard_map/ppermute | solution.py:26
  70.4 6.4 %collective-permute-start.9 = (bf16[2,256,1536]{2,1,0:T(8,128)(2,1)}, bf16[2,256,1536]{2,1,0:T(8,128)(2,1)S(1)}, u32[]{:S(2)}, u32[]{:S(2)}) collective-permute-start(bf16[2,256,1536]{2,1,0:T(8,128)(2,1)} %collective-permute-done.5.refs_7_), channel_id=1, source_target_pairs={{0,1},{1,0},{2,3},{3,2},{4,5},{5,4},{6,7},{7,6},{8,9},{9,8},{10,11... | collective-permute-start | bytes 4718600 | tf_op jit(solution)/shard_map/ppermute | solution.py:26
  145.4 4.3 %collective-permute-start.10 = (f32[2,2,512,128]{3,2,1,0:T(8,128)S(1)}, f32[2,2,512,128]{3,2,1,0:T(8,128)S(1)}, u32[]{:S(2)}, u32[]{:S(2)}) collective-permute-start(f32[2,2,512,128]{3,2,1,0:T(8,128)S(1)} %sum_give.1), channel_id=1, source_target_pairs={{0,1},{1,0},{2,3},{3,2},{4,5},{5,4},{6,7},{7,6},{8,9},{9,8},{10,11... | collective-permute-start | bytes 3145736 | tf_op jit(solution)/shard_map/ppermute | solution.py:26

commit v4 on v3

--- a/solution.py
+++ b/solution.py
@@ -126,7 +126,7 @@
 
     def load_columns(q):
         for p in range(2):
-            start(columns[q].at[p], jv.at[pl.ds(q * HALF, HALF), lanes[1 - p if q == 2 else p]], j_sem)
+            start(columns[q].at[p], jv.at[pl.ds(q * HALF, HALF), lanes[1 - p if q == 2 else p]], j_sem.at[q // 3])
 
     def wait_rows(unit):
         pltpu.make_async_copy(iv.at[unit], iv.at[unit], i_sem.at[unit]).wait()
@@ -150,26 +150,40 @@
         whole = ob.at[unit, pl.ds(first, last - first)]
         pltpu.make_async_copy(whole, whole, out_sem.at[unit]).wait()
 
-    for q in range(slots):
-        load_columns(q)
+    def wait_columns(first, last):
+        ref = jv.at[pl.ds(first * HALF, (last - first) * HALF)]
+        pltpu.make_async_copy(ref, ref, j_sem.at[first // 3]).wait()
+
     if late:
-        for unit in (5, 6, 7, 0, 1, 2, 3, 4):
+        load_columns(3)
+        load_rows(0)
+        load_rows(1)
+        wait_columns(3, 4)
+        for unit in (2, 3, 4):
+            load_rows(unit)
+        for q in range(3):
+            load_columns(q)
+        for unit in (5, 6, 7):
             load_rows(unit)
     else:
+        for q in range(3):
+            load_columns(q)
         for unit in range(5):
             load_rows(unit)
-    pltpu.make_async_copy(jv, jv, j_sem).wait()
+        wait_columns(0, 3)
+
+    @pl.loop(0, 5)
+    def _(unit):
+        wait_rows(unit)
+        multiply(unit, *((3, 4) if late else (0, 3)))
 
     if late:
+        wait_columns(0, 3)
+
         @pl.loop(5, 8)
         def _(unit):
             wait_rows(unit)
             multiply(unit, 0, 4)
-
-    @pl.loop(0, 5)
-    def _(unit):
-        wait_rows(unit)
-        multiply(unit, *((3, 4) if late else (0, 3)))
 
     if late:
         @pl.loop(5, 8)
@@ -197,13 +211,13 @@
                 pltpu.VMEM((slots * HALF, 2 * depth), jnp.bfloat16),
                 pltpu.VMEM((units, slots, STRIPS, HALF, 128), jnp.bfloat16),
                 pltpu.SemaphoreType.DMA((units,)),
-                pltpu.SemaphoreType.DMA,
+                pltpu.SemaphoreType.DMA((2,)),
                 pltpu.SemaphoreType.DMA((units,)),
             ],
         ),
         out_shape=jax.ShapeDtypeStruct((16, STRIPS, ROWS, 128), jnp.bfloat16),
         input_output_aliases={len(ins): 0} if late else {},
-        compiler_params=pltpu.CompilerParams(vmem_limit_bytes=(30 if late else 20) * MIB),
+        compiler_params=pltpu.CompilerParams(vmem_limit_bytes=(28 if late else 18) * MIB),
         cost_estimate=pl.CostEstimate(
             flops=(17 if late else 15) * HALF * HALF * 2 * 2 * depth, bytes_accessed=(units + slots) * ROWS * 2 * depth,
             transcendentals=0,
@@ -212,32 +226,57 @@
     )(place, *ins)
 
 
-def sum_kernel(keep, place_ref, scale_ref, parts, out):
-    core = place_ref[0]
+def total_of(scale_ref, parts, n):
+    total = parts[4 * n].astype(jnp.float32)
+    for j in range(1, 4):
+        total = total + parts[4 * n + j].astype(jnp.float32)
+    return total * scale_ref[0]
+
+
+def give_kernel(place_ref, scale_ref, parts, out):
     for n in range(2):
-        total = parts[4 * n].astype(jnp.float32)
-        for j in range(1, 4):
-            total = total + parts[4 * n + j].astype(jnp.float32)
-        total = total * scale_ref[0]
-        if keep:
-            for j in range(STRIPS):
-                base = n * ROWS + core * HALF + j * 128
-                out[:, pl.ds(pl.multiple_of(base, 128), 128)] = total[j]
-        else:
-            out[n] = total
+        out[n] = total_of(scale_ref, parts, n)
+
+
+def keep_kernel(place_ref, scale_ref, parts, out, held, sem):
+    core, step, steps = place_ref[0], pl.program_id(0), pl.num_programs(0)
+    rows = parts.shape[2]
+
+    def copy(i, n, j):
+        base = pl.multiple_of(n * ROWS + core * HALF + j * 128, 128)
+        where = out.at[pl.ds(pl.multiple_of(i * rows, 128), rows), pl.ds(base, 128)]
+        return pltpu.make_async_copy(held.at[i, n, j], where, sem.at[i, n, j])
+
+    for n in range(2):
+        held[step, n] = total_of(scale_ref, parts, n)
+        for j in range(STRIPS):
+            copy(step, n, j).start()
+
+    @pl.when(step == steps - 1)
+    def _():
+        @pl.loop(0, steps)
+        def _(i):
+            for n in range(2):
+                for j in range(STRIPS):
+                    copy(i, n, j).wait()
 
 
 def aux_sum(keep, place, scale, parts):
     steps = 4
     rows = ROWS // steps
     if keep:
-        out_spec = pl.BlockSpec((rows, 2 * ROWS), lambda i, *_: (i, 0))
+        out_spec = pl.BlockSpec(memory_space=pl.ANY)
         shape = (ROWS, 2 * ROWS)
+        scratch = [
+            pltpu.VMEM((steps, 2, STRIPS, rows, 128), jnp.float32),
+            pltpu.SemaphoreType.DMA((steps, 2, STRIPS)),
+        ]
     else:
         out_spec = pl.BlockSpec((2, STRIPS, rows, 128), lambda i, *_: (0, 0, i, 0))
         shape = (2, STRIPS, ROWS, 128)
+        scratch = []
     return pl.pallas_call(
-        lambda *refs: sum_kernel(keep, *refs),
+        keep_kernel if keep else give_kernel,
         grid_spec=pltpu.PrefetchScalarGridSpec(
             num_scalar_prefetch=2,
             grid=(steps,),
@@ -247,6 +286,7 @@
                 ),
             ],
             out_specs=out_spec,
+            scratch_shapes=scratch,
         ),
         out_shape=jax.ShapeDtypeStruct(shape, jnp.float32),
         compiler_params=pltpu.CompilerParams(vmem_limit_bytes=24 * MIB),
@@ -259,11 +299,13 @@
     core = place_ref[0]
     copies = []
     for n in range(2):
-        for j in range(HALF // 128):
-            base = n * ROWS + (1 - core) * HALF + j * 128
-            copies.append(pltpu.make_async_copy(
-                src.at[n, j], out.at[:, pl.ds(pl.multiple_of(base, 128), 128)], sem.at[n, j]
-            ))
+        for j in range(STRIPS):
+            base = pl.multiple_of(n * ROWS + (1 - core) * HALF + j * 128, 128)
+            for i in range(4):
+                rows = pl.ds(i * (ROWS // 4), ROWS // 4)
+                copies.append(pltpu.make_async_copy(
+                    src.at[n, j, rows], out.at[rows, pl.ds(base, 128)], sem.at[n, j, i]
+                ))
     for copy in copies:
         copy.start()
     for copy in copies:
@@ -278,7 +320,7 @@
             grid=(1,),
             in_specs=[pl.BlockSpec(memory_space=pl.ANY)] * 2,
             out_specs=pl.BlockSpec(memory_space=pl.ANY),
-            scratch_shapes=[pltpu.SemaphoreType.DMA((2, HALF // 128))],
+            scratch_shapes=[pltpu.SemaphoreType.DMA((2, STRIPS, 4))],
         ),
         out_shape=jax.ShapeDtypeStruct((ROWS, 2 * ROWS), jnp.float32),
         input_output_aliases={2: 0},

time: 152 us -> 151 us (level)
  transfers between devices with their start and end apart: 11 -> 11, of which waited for: 6 -> 7; matrix products, arithmetic and copies ran while one was open for 1% -> 1% of each run, Pallas kernels for 9% -> 9%
where the time goes in v4:
time: 151 us; the launch traced here: 150 us
  blocking collectives  54.3 us (36%)
  waiting for transfers between devices  40.6 us (27%)
  Pallas kernels  36.9 us (24%)
  starting transfers between devices  16 us (11%)
  local copies, waits for them, and re-layouts  1.57 us (1%)
    all_to_all x1, blocking collectives, body(): lax.all_to_all(packed, AXES, 0, 0, tiled=True, axis_index_groups=groups)  54.3 us
    ppermute x11, waiting for transfers between devices, permute(): return lax.ppermute(a, AXES, pairs)  40.6 us
    pallas_call x2, Pallas kernels, product(): pl.pallas_call(lambda *refs: product_kernel(late, *refs), grid_spec=pltpu...  23.7 us
    ppermute x11, starting transfers between devices, permute(): return lax.ppermute(a, AXES, pairs)  16 us
    pallas_call x1, Pallas kernels, half_rows(): pl.pallas_call(half_kernel, grid_spec=pltpu.PrefetchScalarGridSpec(num_sc...  8.63 us
  transfers between devices with their start and end apart: 11, of which 7 were waited for; matrix products, arithmetic and copies ran while one was open for 1% of the time, Pallas kernels for 9%

profile of v4, /device:TPU:1, one launch (start us, length us, event | category | flops | bytes accessed | tf_op | source)
XLA Modules:
  0.0 150.4 jit_solution(18015067911688126142)
XLA Ops:
  0.7 8.6 %half_rows.1 = bf16[2,256,1536]{2,1,0:T(8,128)(2,1)} custom-call(s32[32]{0:T(128)} %rows_ref.1, s32[32]{0:T(128)} %cols_ref.1, s32[1]{0:T(128)S(6)} %copy.10.count_ref, bf16[32,24,4096]{2,1,0:T(8,128)(2,1)} %blocks_ref.1, bf16[64,8192]{1,0:T(8,128)(2,1)} %bitcast.5), custom_call_target="tpu_custom_call" | custom-call | flops 2000000000 | bytes 8000000 | tf_op jit(solution)/shard_map/half_rows/pallas_call | solution.py:82
  9.3 1.4 collective-permute-start
  10.7 1.5 fusion
  12.2 1.8 %collective-permute-done = bf16[2,256,1536]{2,1,0:T(8,128)(2,1)S(1)} collective-permute-done((bf16[2,256,1536]{2,1,0:T(8,128)(2,1)}, bf16[2,256,1536]{2,1,0:T(8,128)(2,1)S(1)}, u32[]{:S(2)}, u32[]{:S(2)}) %collective-permute-start) | collective-permute-done | bytes 1572896 | tf_op jit(solution)/shard_map/ppermute | solution.py:26
  14.0 0.1 fusion.1
  14.1 0.1 pad_maximum_fusion.refs_1_.refs_6_.refs_9_
  14.2 1.8 %collective-permute-start.1 = (bf16[2,256,1536]{2,1,0:T(8,128)(2,1)S(1)}, bf16[2,256,1536]{2,1,0:T(8,128)(2,1)}, u32[]{:S(2)}, u32[]{:S(2)}) collective-permute-start(bf16[2,256,1536]{2,1,0:T(8,128)(2,1)S(1)} %pad_maximum_fusion.refs_1_.refs_6_.refs_9_), channel_id=1, source_target_pairs={{0,24},{1,9},{2,26},{3,11},{4,28},{5,13},{6,30},{7,15},{8,0},{9,17... | collective-permute-start | bytes 4718600 | tf_op jit(solution)/shard_map/ppermute | solution.py:26
  16.0 1.3 collective-permute-start.6
  17.3 0.1 pad_maximum_fusion.1.refs_2_
  17.4 1.7 %collective-permute-start.3 = (bf16[2,256,1536]{2,1,0:T(8,128)(2,1)S(1)}, bf16[2,256,1536]{2,1,0:T(8,128)(2,1)}, u32[]{:S(2)}, u32[]{:S(2)}) collective-permute-start(bf16[2,256,1536]{2,1,0:T(8,128)(2,1)S(1)} %pad_maximum_fusion.1.refs_2_), channel_id=1, source_target_pairs={{0,24},{1,9},{2,26},{3,11},{4,28},{5,13},{6,30},{7,15},{8,0},{9,17... | collective-permute-start | bytes 4718600 | tf_op jit(solution)/shard_map/ppermute | solution.py:26
  19.2 1.9 %collective-permute-start.8 = (bf16[2,256,1536]{2,1,0:T(8,128)(2,1)S(1)}, bf16[2,256,1536]{2,1,0:T(8,128)(2,1)}, u32[]{:S(2)}, u32[]{:S(2)}) collective-permute-start(bf16[2,256,1536]{2,1,0:T(8,128)(2,1)S(1)} %pad_maximum_fusion.1.refs_2_), channel_id=1, source_target_pairs={{0,97},{1,32},{2,99},{3,34},{4,101},{5,36},{6,103},{7,38},{8,105},... | collective-permute-start | bytes 4718600 | tf_op jit(solution)/shard_map/ppermute | solution.py:26
  21.0 15.0 %collective-permute-done.1.refs_3_ = bf16[2,256,1536]{2,1,0:T(8,128)(2,1)} collective-permute-done((bf16[2,256,1536]{2,1,0:T(8,128)(2,1)S(1)}, bf16[2,256,1536]{2,1,0:T(8,128)(2,1)}, u32[]{:S(2)}, u32[]{:S(2)}) %collective-permute-start.1) | collective-permute-done | bytes 1572896 | tf_op jit(solution)/shard_map/ppermute | solution.py:26
  36.0 0.7 collective-permute-start.2
  36.7 0.0 collective-permute-done.6.refs_7_.refs_10_
  36.7 1.3 collective-permute-start.7
  38.0 0.6 collective-permute-start.5
  38.6 0.1 pad_add_fusion.refs_0_.place_ref
  38.7 14.5 %collective-permute-done.3.refs_5_ = bf16[2,256,1536]{2,1,0:T(8,128)(2,1)} collective-permute-done((bf16[2,256,1536]{2,1,0:T(8,128)(2,1)S(1)}, bf16[2,256,1536]{2,1,0:T(8,128)(2,1)}, u32[]{:S(2)}, u32[]{:S(2)}) %collective-permute-start.3) | collective-permute-done | bytes 1572896 | tf_op jit(solution)/shard_map/ppermute | solution.py:26
  53.2 0.4 collective-permute-start.4
  53.6 2.2 %collective-permute-done.8.refs_8_.refs_11_ = bf16[2,256,1536]{2,1,0:T(8,128)(2,1)} collective-permute-done((bf16[2,256,1536]{2,1,0:T(8,128)(2,1)S(1)}, bf16[2,256,1536]{2,1,0:T(8,128)(2,1)}, u32[]{:S(2)}, u32[]{:S(2)}) %collective-permute-start.8) | collective-permute-done | bytes 1572896 | tf_op jit(solution)/shard_map/ppermute | solution.py:26
  55.8 0.0 collective-permute-done.2.refs_4_
  55.8 11.1 %product_early.1.refs_13_ = bf16[16,2,512,128]{3,2,1,0:T(8,128)(2,1)S(1)} custom-call(s32[4]{0:T(128)S(1)} %pad_add_fusion.refs_0_.place_ref, bf16[2,256,1536]{2,1,0:T(8,128)(2,1)S(1)} %pad_maximum_fusion.refs_1_.refs_6_.refs_9_, bf16[2,256,1536]{2,1,0:T(8,128)(2,1)S(1)} %pad_maximum_fusion.1.refs_2_, bf16[2,256,1536]{2,1,0:T(8,128)(2,1)} %collective-permute-done.1.refs_3_, ...), custom_call_target="tpu_custom_call" | custom-call | flops 6039797760 | bytes 12582912 | tf_op jit(solution)/shard_map/product_early/pallas_call | solution.py:202
  66.9 3.5 %collective-permute-done.7.refs_12_ = bf16[2,256,1536]{2,1,0:T(8,128)(2,1)} collective-permute-done((bf16[2,256,1536]{2,1,0:T(8,128)(2,1)}, bf16[2,256,1536]{2,1,0:T(8,128)(2,1)}, u32[]{:S(2)}, u32[]{:S(2)}) %collective-permute-start.7) | collective-permute-done | bytes 1572896 | tf_op jit(solution)/shard_map/ppermute | solution.py:26
  70.4 0.0 collective-permute-done.5.refs_7_
  70.4 3.2 %collective-permute-start.9 = (bf16[2,256,1536]{2,1,0:T(8,128)(2,1)}, bf16[2,256,1536]{2,1,0:T(8,128)(2,1)S(1)}, u32[]{:S(2)}, u32[]{:S(2)}) collective-permute-start(bf16[2,256,1536]{2,1,0:T(8,128)(2,1)} %collective-permute-done.5.refs_7_), channel_id=1, source_target_pairs={{0,1},{1,0},{2,3},{3,2},{4,5},{5,4},{6,7},{7,6},{8,9},{9,8},{10,11... | collective-permute-start | bytes 4718600 | tf_op jit(solution)/shard_map/ppermute | solution.py:26
  73.5 0.0 collective-permute-done.4.refs_6_
  73.5 3.2 %collective-permute-done.9.refs_8_ = bf16[2,256,1536]{2,1,0:T(8,128)(2,1)S(1)} collective-permute-done((bf16[2,256,1536]{2,1,0:T(8,128)(2,1)}, bf16[2,256,1536]{2,1,0:T(8,128)(2,1)S(1)}, u32[]{:S(2)}, u32[]{:S(2)}) %collective-permute-start.9) | collective-permute-done | bytes 1572896 | tf_op jit(solution)/shard_map/ppermute | solution.py:26
  76.8 12.5 %product_late.1 = bf16[16,2,512,128]{3,2,1,0:T(8,128)(2,1)S(1)} custom-call(s32[4]{0:T(128)S(1)} %pad_add_fusion.refs_0_.place_ref, bf16[2,256,1536]{2,1,0:T(8,128)(2,1)S(1)} %pad_maximum_fusion.refs_1_.refs_6_.refs_9_, bf16[2,256,1536]{2,1,0:T(8,128)(2,1)S(1)} %pad_maximum_fusion.1.refs_2_, ...), custom_call_target="tpu_custom_call", output_to_operand_aliasing={{}: (13, {})} | custom-call | flops 6845104128 | bytes 18874368 | tf_op jit(solution)/shard_map/product_late/pallas_call | solution.py:202
  89.3 54.3 %all_to_all.5.parts = bf16[16,2,512,128]{3,2,1,0:T(8,128)(2,1)S(1)} all-to-all(bf16[16,2,512,128]{3,2,1,0:T(8,128)(2,1)S(1)} %product_late.1), channel_id=1, replica_groups={{0,2,4,6,8,10,12,14,16,18,20,22,24,26,28,30},{1,3,5,7,9,11,13,15,17,19,..., dimensions={0} | all-to-all | bytes 8388608 | tf_op jit(solution)/shard_map/all_to_all | solution.py:368
  143.6 1.1 sum_give.1
  144.8 1.7 %collective-permute-start.10 = (f32[2,2,512,128]{3,2,1,0:T(8,128)S(1)}, f32[2,2,512,128]{3,2,1,0:T(8,128)S(1)}, u32[]{:S(2)}, u32[]{:S(2)}) collective-permute-start(f32[2,2,512,128]{3,2,1,0:T(8,128)S(1)} %sum_give.1), channel_id=1, source_target_pairs={{0,1},{1,0},{2,3},{3,2},{4,5},{5,4},{6,7},{7,6},{8,9},{9,8},{10,11... | collective-permute-start | bytes 3145736 | tf_op jit(solution)/shard_map/ppermute | solution.py:26
  146.5 1.9 %sum_keep.1.before = f32[512,1024]{1,0:T(8,128)} custom-call(s32[4]{0:T(128)S(1)} %pad_add_fusion.refs_0_.place_ref, f32[1]{0:T(128)} %constant.16.clone.1.scale_ref, bf16[16,2,512,128]{3,2,1,0:T(8,128)(2,1)S(1)} %all_to_all.5.parts), custom_call_target="tpu_custom_call" | custom-call | flops 2097152 | bytes 6291456 | tf_op jit(solution)/shard_map/sum_keep/pallas_call | solution.py:278
  148.4 0.4 collective-permute-done.10.src
  148.8 1.6 %assemble.1 = f32[512,1024]{1,0:T(8,128)} custom-call(s32[4]{0:T(128)S(1)} %pad_add_fusion.refs_0_.place_ref, f32[2,2,512,128]{3,2,1,0:T(8,128)S(1)} %collective-permute-done.10.src, f32[512,1024]{1,0:T(8,128)} %sum_keep.1.before), custom_call_target="tpu_custom_call", output_to_operand_aliasing={{}: (2, {})} | custom-call | tf_op jit(solution)/shard_map/assemble/pallas_call | solution.py:316
Async XLA Ops:
  9.3 4.7 %collective-permute-start = (bf16[2,256,1536]{2,1,0:T(8,128)(2,1)}, bf16[2,256,1536]{2,1,0:T(8,128)(2,1)S(1)}, u32[]{:S(2)}, u32[]{:S(2)}) collective-permute-start(bf16[2,256,1536]{2,1,0:T(8,128)(2,1)} %half_rows.1), channel_id=1, source_target_pairs={{0,1},{1,0},{2,3},{3,2},{4,5},{5,4},{6,7},{7,6},{8,9},{9,8},{10,11... | collective-permute-start | bytes 4718600 | tf_op jit(solution)/shard_map/ppermute | solution.py:26
  14.2 21.8 %collective-permute-start.1 = (bf16[2,256,1536]{2,1,0:T(8,128)(2,1)S(1)}, bf16[2,256,1536]{2,1,0:T(8,128)(2,1)}, u32[]{:S(2)}, u32[]{:S(2)}) collective-permute-start(bf16[2,256,1536]{2,1,0:T(8,128)(2,1)S(1)} %pad_maximum_fusion.refs_1_.refs_6_.refs_9_), channel_id=1, source_target_pairs={{0,24},{1,9},{2,26},{3,11},{4,28},{5,13},{6,30},{7,15},{8,0},{9,17... | collective-permute-start | bytes 4718600 | tf_op jit(solution)/shard_map/ppermute | solution.py:26
  16.0 20.7 %collective-permute-start.6 = (bf16[2,256,1536]{2,1,0:T(8,128)(2,1)S(1)}, bf16[2,256,1536]{2,1,0:T(8,128)(2,1)}, u32[]{:S(2)}, u32[]{:S(2)}) collective-permute-start(bf16[2,256,1536]{2,1,0:T(8,128)(2,1)S(1)} %pad_maximum_fusion.refs_1_.refs_6_.refs_9_), channel_id=1, source_target_pairs={{0,96},{1,33},{2,98},{3,35},{4,100},{5,37},{6,102},{7,39},{8,104},... | collective-permute-start | bytes 4718600 | tf_op jit(solution)/shard_map/ppermute | solution.py:26
  17.4 35.7 %collective-permute-start.3 = (bf16[2,256,1536]{2,1,0:T(8,128)(2,1)S(1)}, bf16[2,256,1536]{2,1,0:T(8,128)(2,1)}, u32[]{:S(2)}, u32[]{:S(2)}) collective-permute-start(bf16[2,256,1536]{2,1,0:T(8,128)(2,1)S(1)} %pad_maximum_fusion.1.refs_2_), channel_id=1, source_target_pairs={{0,24},{1,9},{2,26},{3,11},{4,28},{5,13},{6,30},{7,15},{8,0},{9,17... | collective-permute-start | bytes 4718600 | tf_op jit(solution)/shard_map/ppermute | solution.py:26
  19.2 36.6 %collective-permute-start.8 = (bf16[2,256,1536]{2,1,0:T(8,128)(2,1)S(1)}, bf16[2,256,1536]{2,1,0:T(8,128)(2,1)}, u32[]{:S(2)}, u32[]{:S(2)}) collective-permute-start(bf16[2,256,1536]{2,1,0:T(8,128)(2,1)S(1)} %pad_maximum_fusion.1.refs_2_), channel_id=1, source_target_pairs={{0,97},{1,32},{2,99},{3,34},{4,101},{5,36},{6,103},{7,38},{8,105},... | collective-permute-start | bytes 4718600 | tf_op jit(solution)/shard_map/ppermute | solution.py:26
  36.0 19.7 %collective-permute-start.2 = (bf16[2,256,1536]{2,1,0:T(8,128)(2,1)}, bf16[2,256,1536]{2,1,0:T(8,128)(2,1)}, u32[]{:S(2)}, u32[]{:S(2)}) collective-permute-start(bf16[2,256,1536]{2,1,0:T(8,128)(2,1)} %collective-permute-done.1.refs_3_), channel_id=1, source_target_pairs={{0,1},{1,0},{2,3},{3,2},{4,5},{5,4},{6,7},{7,6},{8,9},{9,8},{10,11... | collective-permute-start | bytes 4718600 | tf_op jit(solution)/shard_map/ppermute | solution.py:26
  36.7 33.6 %collective-permute-start.7 = (bf16[2,256,1536]{2,1,0:T(8,128)(2,1)}, bf16[2,256,1536]{2,1,0:T(8,128)(2,1)}, u32[]{:S(2)}, u32[]{:S(2)}) collective-permute-start(bf16[2,256,1536]{2,1,0:T(8,128)(2,1)} %collective-permute-done.6.refs_7_.refs_10_), channel_id=1, source_target_pairs={{0,96},{1,33},{2,98},{3,35},{4,100},{5,37},{6,102},{7,39},{8,104},... | collective-permute-start | bytes 4718600 | tf_op jit(solution)/shard_map/ppermute | solution.py:26
  38.0 32.3 %collective-permute-start.5 = (bf16[2,256,1536]{2,1,0:T(8,128)(2,1)}, bf16[2,256,1536]{2,1,0:T(8,128)(2,1)}, u32[]{:S(2)}, u32[]{:S(2)}) collective-permute-start(bf16[2,256,1536]{2,1,0:T(8,128)(2,1)} %collective-permute-done.1.refs_3_), channel_id=1, source_target_pairs={{0,24},{1,9},{2,26},{3,11},{4,28},{5,13},{6,30},{7,15},{8,0},{9,17... | collective-permute-start | bytes 4718600 | tf_op jit(solution)/shard_map/ppermute | solution.py:26
  53.2 20.4 %collective-permute-start.4 = (bf16[2,256,1536]{2,1,0:T(8,128)(2,1)}, bf16[2,256,1536]{2,1,0:T(8,128)(2,1)S(1)}, u32[]{:S(2)}, u32[]{:S(2)}) collective-permute-start(bf16[2,256,1536]{2,1,0:T(8,128)(2,1)} %collective-permute-done.3.refs_5_), channel_id=1, source_target_pairs={{0,1},{1,0},{2,3},{3,2},{4,5},{5,4},{6,7},{7,6},{8,9},{9,8},{10,11... | collective-permute-start | bytes 4718600 | tf_op jit(solution)/shard_map/ppermute | solution.py:26
  70.4 6.4 %collective-permute-start.9 = (bf16[2,256,1536]{2,1,0:T(8,128)(2,1)}, bf16[2,256,1536]{2,1,0:T(8,128)(2,1)S(1)}, u32[]{:S(2)}, u32[]{:S(2)}) collective-permute-start(bf16[2,256,1536]{2,1,0:T(8,128)(2,1)} %collective-permute-done.5.refs_7_), channel_id=1, source_target_pairs={{0,1},{1,0},{2,3},{3,2},{4,5},{5,4},{6,7},{7,6},{8,9},{9,8},{10,11... | collective-permute-start | bytes 4718600 | tf_op jit(solution)/shard_map/ppermute | solution.py:26
  144.8 4.0 %collective-permute-start.10 = (f32[2,2,512,128]{3,2,1,0:T(8,128)S(1)}, f32[2,2,512,128]{3,2,1,0:T(8,128)S(1)}, u32[]{:S(2)}, u32[]{:S(2)}) collective-permute-start(f32[2,2,512,128]{3,2,1,0:T(8,128)S(1)} %sum_give.1), channel_id=1, source_target_pairs={{0,1},{1,0},{2,3},{3,2},{4,5},{5,4},{6,7},{7,6},{8,9},{9,8},{10,11... | collective-permute-start | bytes 3145736 | tf_op jit(solution)/shard_map/ppermute | solution.py:26

commit v5 on v4

--- a/solution.py
+++ b/solution.py
@@ -51,10 +51,10 @@
         coeff = jnp.concatenate(
             [jnp.where(lane < 64, left, 0.0), jnp.where(lane < 64, 0.0, right)], axis=0
         ).astype(jnp.bfloat16)
-        x = blocks_ref[j].astype(jnp.float32)
+        x = blocks_ref[j]
         x = jnp.concatenate([x[:, t * 128:(t + 1) * 128] for t in range(tiles)], axis=0)
         prod = lax.dot_general(
-            x.astype(jnp.bfloat16), coeff, (((1,), (1,)), ((), ())), preferred_element_type=jnp.float32
+            x, coeff, (((1,), (1,)), ((), ())), preferred_element_type=jnp.float32
         )
         acc[rows_ref[s]] += prod
 

time: 151 us -> 151 us (level)
  no operation moved by 1% of the time
where the time goes in v5:
time: 151 us; the launch traced here: 150 us
  blocking collectives  54.3 us (36%)
  waiting for transfers between devices  40.6 us (27%)
  Pallas kernels  36.9 us (24%)
  starting transfers between devices  16 us (11%)
  local copies, waits for them, and re-layouts  1.57 us (1%)
    all_to_all x1, blocking collectives, body(): lax.all_to_all(packed, AXES, 0, 0, tiled=True, axis_index_groups=groups)  54.3 us
    ppermute x11, waiting for transfers between devices, permute(): return lax.ppermute(a, AXES, pairs)  40.6 us
    pallas_call x2, Pallas kernels, product(): pl.pallas_call(lambda *refs: product_kernel(late, *refs), grid_spec=pltpu...  23.7 us
    ppermute x11, starting transfers between devices, permute(): return lax.ppermute(a, AXES, pairs)  16 us
    pallas_call x1, Pallas kernels, half_rows(): pl.pallas_call(half_kernel, grid_spec=pltpu.PrefetchScalarGridSpec(num_sc...  8.63 us
  transfers between devices with their start and end apart: 11, of which 7 were waited for; matrix products, arithmetic and copies ran while one was open for 1% of the time, Pallas kernels for 9%

profile of v5, /device:TPU:1, one launch (start us, length us, event | category | flops | bytes accessed | tf_op | source)
XLA Modules:
  0.0 150.4 jit_solution(16180437670895504857)
XLA Ops:
  0.7 8.6 %half_rows.1 = bf16[2,256,1536]{2,1,0:T(8,128)(2,1)} custom-call(s32[32]{0:T(128)} %rows_ref.1, s32[32]{0:T(128)} %cols_ref.1, s32[1]{0:T(128)S(6)} %copy.10.count_ref, bf16[32,24,4096]{2,1,0:T(8,128)(2,1)} %blocks_ref.1, bf16[64,8192]{1,0:T(8,128)(2,1)} %bitcast.5), custom_call_target="tpu_custom_call" | custom-call | flops 2000000000 | bytes 8000000 | tf_op jit(solution)/shard_map/half_rows/pallas_call | solution.py:82
  9.3 1.4 collective-permute-start
  10.7 1.5 fusion
  12.2 1.8 %collective-permute-done = bf16[2,256,1536]{2,1,0:T(8,128)(2,1)S(1)} collective-permute-done((bf16[2,256,1536]{2,1,0:T(8,128)(2,1)}, bf16[2,256,1536]{2,1,0:T(8,128)(2,1)S(1)}, u32[]{:S(2)}, u32[]{:S(2)}) %collective-permute-start) | collective-permute-done | bytes 1572896 | tf_op jit(solution)/shard_map/ppermute | solution.py:26
  14.0 0.1 fusion.1
  14.1 0.1 pad_maximum_fusion.refs_1_.refs_6_.refs_9_
  14.2 1.8 %collective-permute-start.1 = (bf16[2,256,1536]{2,1,0:T(8,128)(2,1)S(1)}, bf16[2,256,1536]{2,1,0:T(8,128)(2,1)}, u32[]{:S(2)}, u32[]{:S(2)}) collective-permute-start(bf16[2,256,1536]{2,1,0:T(8,128)(2,1)S(1)} %pad_maximum_fusion.refs_1_.refs_6_.refs_9_), channel_id=1, source_target_pairs={{0,24},{1,9},{2,26},{3,11},{4,28},{5,13},{6,30},{7,15},{8,0},{9,17... | collective-permute-start | bytes 4718600 | tf_op jit(solution)/shard_map/ppermute | solution.py:26
  16.0 1.3 collective-permute-start.6
  17.3 0.1 pad_maximum_fusion.1.refs_2_
  17.4 1.7 %collective-permute-start.3 = (bf16[2,256,1536]{2,1,0:T(8,128)(2,1)S(1)}, bf16[2,256,1536]{2,1,0:T(8,128)(2,1)}, u32[]{:S(2)}, u32[]{:S(2)}) collective-permute-start(bf16[2,256,1536]{2,1,0:T(8,128)(2,1)S(1)} %pad_maximum_fusion.1.refs_2_), channel_id=1, source_target_pairs={{0,24},{1,9},{2,26},{3,11},{4,28},{5,13},{6,30},{7,15},{8,0},{9,17... | collective-permute-start | bytes 4718600 | tf_op jit(solution)/shard_map/ppermute | solution.py:26
  19.2 1.9 %collective-permute-start.8 = (bf16[2,256,1536]{2,1,0:T(8,128)(2,1)S(1)}, bf16[2,256,1536]{2,1,0:T(8,128)(2,1)}, u32[]{:S(2)}, u32[]{:S(2)}) collective-permute-start(bf16[2,256,1536]{2,1,0:T(8,128)(2,1)S(1)} %pad_maximum_fusion.1.refs_2_), channel_id=1, source_target_pairs={{0,97},{1,32},{2,99},{3,34},{4,101},{5,36},{6,103},{7,38},{8,105},... | collective-permute-start | bytes 4718600 | tf_op jit(solution)/shard_map/ppermute | solution.py:26
  21.0 15.0 %collective-permute-done.1.refs_3_ = bf16[2,256,1536]{2,1,0:T(8,128)(2,1)} collective-permute-done((bf16[2,256,1536]{2,1,0:T(8,128)(2,1)S(1)}, bf16[2,256,1536]{2,1,0:T(8,128)(2,1)}, u32[]{:S(2)}, u32[]{:S(2)}) %collective-permute-start.1) | collective-permute-done | bytes 1572896 | tf_op jit(solution)/shard_map/ppermute | solution.py:26
  36.0 0.7 collective-permute-start.2
  36.7 0.0 collective-permute-done.6.refs_7_.refs_10_
  36.7 1.3 collective-permute-start.7
  38.0 0.6 collective-permute-start.5
  38.6 0.1 pad_add_fusion.refs_0_.place_ref
  38.7 14.5 %collective-permute-done.3.refs_5_ = bf16[2,256,1536]{2,1,0:T(8,128)(2,1)} collective-permute-done((bf16[2,256,1536]{2,1,0:T(8,128)(2,1)S(1)}, bf16[2,256,1536]{2,1,0:T(8,128)(2,1)}, u32[]{:S(2)}, u32[]{:S(2)}) %collective-permute-start.3) | collective-permute-done | bytes 1572896 | tf_op jit(solution)/shard_map/ppermute | solution.py:26
  53.2 0.4 collective-permute-start.4
  53.6 2.2 %collective-permute-done.8.refs_8_.refs_11_ = bf16[2,256,1536]{2,1,0:T(8,128)(2,1)} collective-permute-done((bf16[2,256,1536]{2,1,0:T(8,128)(2,1)S(1)}, bf16[2,256,1536]{2,1,0:T(8,128)(2,1)}, u32[]{:S(2)}, u32[]{:S(2)}) %collective-permute-start.8) | collective-permute-done | bytes 1572896 | tf_op jit(solution)/shard_map/ppermute | solution.py:26
  55.8 0.0 collective-permute-done.2.refs_4_
  55.8 11.1 %product_early.1.refs_13_ = bf16[16,2,512,128]{3,2,1,0:T(8,128)(2,1)S(1)} custom-call(s32[4]{0:T(128)S(1)} %pad_add_fusion.refs_0_.place_ref, bf16[2,256,1536]{2,1,0:T(8,128)(2,1)S(1)} %pad_maximum_fusion.refs_1_.refs_6_.refs_9_, bf16[2,256,1536]{2,1,0:T(8,128)(2,1)S(1)} %pad_maximum_fusion.1.refs_2_, bf16[2,256,1536]{2,1,0:T(8,128)(2,1)} %collective-permute-done.1.refs_3_, ...), custom_call_target="tpu_custom_call" | custom-call | flops 6039797760 | bytes 12582912 | tf_op jit(solution)/shard_map/product_early/pallas_call | solution.py:202
  66.9 3.5 %collective-permute-done.7.refs_12_ = bf16[2,256,1536]{2,1,0:T(8,128)(2,1)} collective-permute-done((bf16[2,256,1536]{2,1,0:T(8,128)(2,1)}, bf16[2,256,1536]{2,1,0:T(8,128)(2,1)}, u32[]{:S(2)}, u32[]{:S(2)}) %collective-permute-start.7) | collective-permute-done | bytes 1572896 | tf_op jit(solution)/shard_map/ppermute | solution.py:26
  70.4 0.0 collective-permute-done.5.refs_7_
  70.4 3.2 %collective-permute-start.9 = (bf16[2,256,1536]{2,1,0:T(8,128)(2,1)}, bf16[2,256,1536]{2,1,0:T(8,128)(2,1)S(1)}, u32[]{:S(2)}, u32[]{:S(2)}) collective-permute-start(bf16[2,256,1536]{2,1,0:T(8,128)(2,1)} %collective-permute-done.5.refs_7_), channel_id=1, source_target_pairs={{0,1},{1,0},{2,3},{3,2},{4,5},{5,4},{6,7},{7,6},{8,9},{9,8},{10,11... | collective-permute-start | bytes 4718600 | tf_op jit(solution)/shard_map/ppermute | solution.py:26
  73.5 0.0 collective-permute-done.4.refs_6_
  73.5 3.2 %collective-permute-done.9.refs_8_ = bf16[2,256,1536]{2,1,0:T(8,128)(2,1)S(1)} collective-permute-done((bf16[2,256,1536]{2,1,0:T(8,128)(2,1)}, bf16[2,256,1536]{2,1,0:T(8,128)(2,1)S(1)}, u32[]{:S(2)}, u32[]{:S(2)}) %collective-permute-start.9) | collective-permute-done | bytes 1572896 | tf_op jit(solution)/shard_map/ppermute | solution.py:26
  76.8 12.5 %product_late.1 = bf16[16,2,512,128]{3,2,1,0:T(8,128)(2,1)S(1)} custom-call(s32[4]{0:T(128)S(1)} %pad_add_fusion.refs_0_.place_ref, bf16[2,256,1536]{2,1,0:T(8,128)(2,1)S(1)} %pad_maximum_fusion.refs_1_.refs_6_.refs_9_, bf16[2,256,1536]{2,1,0:T(8,128)(2,1)S(1)} %pad_maximum_fusion.1.refs_2_, ...), custom_call_target="tpu_custom_call", output_to_operand_aliasing={{}: (13, {})} | custom-call | flops 6845104128 | bytes 18874368 | tf_op jit(solution)/shard_map/product_late/pallas_call | solution.py:202
  89.3 54.3 %all_to_all.5.parts = bf16[16,2,512,128]{3,2,1,0:T(8,128)(2,1)S(1)} all-to-all(bf16[16,2,512,128]{3,2,1,0:T(8,128)(2,1)S(1)} %product_late.1), channel_id=1, replica_groups={{0,2,4,6,8,10,12,14,16,18,20,22,24,26,28,30},{1,3,5,7,9,11,13,15,17,19,..., dimensions={0} | all-to-all | bytes 8388608 | tf_op jit(solution)/shard_map/all_to_all | solution.py:368
  143.6 1.1 sum_give.1
  144.7 1.8 %collective-permute-start.10 = (f32[2,2,512,128]{3,2,1,0:T(8,128)S(1)}, f32[2,2,512,128]{3,2,1,0:T(8,128)S(1)}, u32[]{:S(2)}, u32[]{:S(2)}) collective-permute-start(f32[2,2,512,128]{3,2,1,0:T(8,128)S(1)} %sum_give.1), channel_id=1, source_target_pairs={{0,1},{1,0},{2,3},{3,2},{4,5},{5,4},{6,7},{7,6},{8,9},{9,8},{10,11... | collective-permute-start | bytes 3145736 | tf_op jit(solution)/shard_map/ppermute | solution.py:26
  146.5 1.9 %sum_keep.1.before = f32[512,1024]{1,0:T(8,128)} custom-call(s32[4]{0:T(128)S(1)} %pad_add_fusion.refs_0_.place_ref, f32[1]{0:T(128)} %constant.16.clone.1.scale_ref, bf16[16,2,512,128]{3,2,1,0:T(8,128)(2,1)S(1)} %all_to_all.5.parts), custom_call_target="tpu_custom_call" | custom-call | flops 2097152 | bytes 6291456 | tf_op jit(solution)/shard_map/sum_keep/pallas_call | solution.py:278
  148.4 0.4 collective-permute-done.10.src
  148.8 1.6 %assemble.1 = f32[512,1024]{1,0:T(8,128)} custom-call(s32[4]{0:T(128)S(1)} %pad_add_fusion.refs_0_.place_ref, f32[2,2,512,128]{3,2,1,0:T(8,128)S(1)} %collective-permute-done.10.src, f32[512,1024]{1,0:T(8,128)} %sum_keep.1.before), custom_call_target="tpu_custom_call", output_to_operand_aliasing={{}: (2, {})} | custom-call | tf_op jit(solution)/shard_map/assemble/pallas_call | solution.py:316
Async XLA Ops:
  9.3 4.7 %collective-permute-start = (bf16[2,256,1536]{2,1,0:T(8,128)(2,1)}, bf16[2,256,1536]{2,1,0:T(8,128)(2,1)S(1)}, u32[]{:S(2)}, u32[]{:S(2)}) collective-permute-start(bf16[2,256,1536]{2,1,0:T(8,128)(2,1)} %half_rows.1), channel_id=1, source_target_pairs={{0,1},{1,0},{2,3},{3,2},{4,5},{5,4},{6,7},{7,6},{8,9},{9,8},{10,11... | collective-permute-start | bytes 4718600 | tf_op jit(solution)/shard_map/ppermute | solution.py:26
  14.2 21.8 %collective-permute-start.1 = (bf16[2,256,1536]{2,1,0:T(8,128)(2,1)S(1)}, bf16[2,256,1536]{2,1,0:T(8,128)(2,1)}, u32[]{:S(2)}, u32[]{:S(2)}) collective-permute-start(bf16[2,256,1536]{2,1,0:T(8,128)(2,1)S(1)} %pad_maximum_fusion.refs_1_.refs_6_.refs_9_), channel_id=1, source_target_pairs={{0,24},{1,9},{2,26},{3,11},{4,28},{5,13},{6,30},{7,15},{8,0},{9,17... | collective-permute-start | bytes 4718600 | tf_op jit(solution)/shard_map/ppermute | solution.py:26
  16.0 20.7 %collective-permute-start.6 = (bf16[2,256,1536]{2,1,0:T(8,128)(2,1)S(1)}, bf16[2,256,1536]{2,1,0:T(8,128)(2,1)}, u32[]{:S(2)}, u32[]{:S(2)}) collective-permute-start(bf16[2,256,1536]{2,1,0:T(8,128)(2,1)S(1)} %pad_maximum_fusion.refs_1_.refs_6_.refs_9_), channel_id=1, source_target_pairs={{0,96},{1,33},{2,98},{3,35},{4,100},{5,37},{6,102},{7,39},{8,104},... | collective-permute-start | bytes 4718600 | tf_op jit(solution)/shard_map/ppermute | solution.py:26
  17.4 35.7 %collective-permute-start.3 = (bf16[2,256,1536]{2,1,0:T(8,128)(2,1)S(1)}, bf16[2,256,1536]{2,1,0:T(8,128)(2,1)}, u32[]{:S(2)}, u32[]{:S(2)}) collective-permute-start(bf16[2,256,1536]{2,1,0:T(8,128)(2,1)S(1)} %pad_maximum_fusion.1.refs_2_), channel_id=1, source_target_pairs={{0,24},{1,9},{2,26},{3,11},{4,28},{5,13},{6,30},{7,15},{8,0},{9,17... | collective-permute-start | bytes 4718600 | tf_op jit(solution)/shard_map/ppermute | solution.py:26
  19.2 36.6 %collective-permute-start.8 = (bf16[2,256,1536]{2,1,0:T(8,128)(2,1)S(1)}, bf16[2,256,1536]{2,1,0:T(8,128)(2,1)}, u32[]{:S(2)}, u32[]{:S(2)}) collective-permute-start(bf16[2,256,1536]{2,1,0:T(8,128)(2,1)S(1)} %pad_maximum_fusion.1.refs_2_), channel_id=1, source_target_pairs={{0,97},{1,32},{2,99},{3,34},{4,101},{5,36},{6,103},{7,38},{8,105},... | collective-permute-start | bytes 4718600 | tf_op jit(solution)/shard_map/ppermute | solution.py:26
  36.0 19.7 %collective-permute-start.2 = (bf16[2,256,1536]{2,1,0:T(8,128)(2,1)}, bf16[2,256,1536]{2,1,0:T(8,128)(2,1)}, u32[]{:S(2)}, u32[]{:S(2)}) collective-permute-start(bf16[2,256,1536]{2,1,0:T(8,128)(2,1)} %collective-permute-done.1.refs_3_), channel_id=1, source_target_pairs={{0,1},{1,0},{2,3},{3,2},{4,5},{5,4},{6,7},{7,6},{8,9},{9,8},{10,11... | collective-permute-start | bytes 4718600 | tf_op jit(solution)/shard_map/ppermute | solution.py:26
  36.7 33.6 %collective-permute-start.7 = (bf16[2,256,1536]{2,1,0:T(8,128)(2,1)}, bf16[2,256,1536]{2,1,0:T(8,128)(2,1)}, u32[]{:S(2)}, u32[]{:S(2)}) collective-permute-start(bf16[2,256,1536]{2,1,0:T(8,128)(2,1)} %collective-permute-done.6.refs_7_.refs_10_), channel_id=1, source_target_pairs={{0,96},{1,33},{2,98},{3,35},{4,100},{5,37},{6,102},{7,39},{8,104},... | collective-permute-start | bytes 4718600 | tf_op jit(solution)/shard_map/ppermute | solution.py:26
  38.0 32.3 %collective-permute-start.5 = (bf16[2,256,1536]{2,1,0:T(8,128)(2,1)}, bf16[2,256,1536]{2,1,0:T(8,128)(2,1)}, u32[]{:S(2)}, u32[]{:S(2)}) collective-permute-start(bf16[2,256,1536]{2,1,0:T(8,128)(2,1)} %collective-permute-done.1.refs_3_), channel_id=1, source_target_pairs={{0,24},{1,9},{2,26},{3,11},{4,28},{5,13},{6,30},{7,15},{8,0},{9,17... | collective-permute-start | bytes 4718600 | tf_op jit(solution)/shard_map/ppermute | solution.py:26
  53.2 20.4 %collective-permute-start.4 = (bf16[2,256,1536]{2,1,0:T(8,128)(2,1)}, bf16[2,256,1536]{2,1,0:T(8,128)(2,1)S(1)}, u32[]{:S(2)}, u32[]{:S(2)}) collective-permute-start(bf16[2,256,1536]{2,1,0:T(8,128)(2,1)} %collective-permute-done.3.refs_5_), channel_id=1, source_target_pairs={{0,1},{1,0},{2,3},{3,2},{4,5},{5,4},{6,7},{7,6},{8,9},{9,8},{10,11... | collective-permute-start | bytes 4718600 | tf_op jit(solution)/shard_map/ppermute | solution.py:26
  70.4 6.4 %collective-permute-start.9 = (bf16[2,256,1536]{2,1,0:T(8,128)(2,1)}, bf16[2,256,1536]{2,1,0:T(8,128)(2,1)S(1)}, u32[]{:S(2)}, u32[]{:S(2)}) collective-permute-start(bf16[2,256,1536]{2,1,0:T(8,128)(2,1)} %collective-permute-done.5.refs_7_), channel_id=1, source_target_pairs={{0,1},{1,0},{2,3},{3,2},{4,5},{5,4},{6,7},{7,6},{8,9},{9,8},{10,11... | collective-permute-start | bytes 4718600 | tf_op jit(solution)/shard_map/ppermute | solution.py:26
  144.7 4.0 %collective-permute-start.10 = (f32[2,2,512,128]{3,2,1,0:T(8,128)S(1)}, f32[2,2,512,128]{3,2,1,0:T(8,128)S(1)}, u32[]{:S(2)}, u32[]{:S(2)}) collective-permute-start(f32[2,2,512,128]{3,2,1,0:T(8,128)S(1)} %sum_give.1), channel_id=1, source_target_pairs={{0,1},{1,0},{2,3},{3,2},{4,5},{5,4},{6,7},{7,6},{8,9},{9,8},{10,11... | collective-permute-start | bytes 3145736 | tf_op jit(solution)/shard_map/ppermute | solution.py:26

commit v6 on v4

--- a/solution.py
+++ b/solution.py
@@ -131,10 +131,14 @@
     def wait_rows(unit):
         pltpu.make_async_copy(iv.at[unit], iv.at[unit], i_sem.at[unit]).wait()
 
-    def multiply(unit, first, last):
-        result = lax.dot_general(
-            iv[unit], jv[first * HALF:last * HALF, :], (((1,), (1,)), ((), ())), preferred_element_type=jnp.float32
+    def product_of(left, first, last):
+        return lax.dot_general(
+            left, jv[first * HALF:last * HALF, :], (((1,), (1,)), ((), ())), preferred_element_type=jnp.float32
         )
+
+    def multiply(unit, first, last, result=None):
+        if result is None:
+            result = product_of(iv[unit], first, last)
         slot = jnp.where(unit < 2, 0, jnp.where(unit >= 6, 3, jnp.where(unit % 2 == 1, 2, 1)))
         mine = jnp.logical_or(unit == 0, jnp.logical_or(unit == 2, jnp.logical_or(unit == 5, unit == 6)))
         span = pl.ds(pl.multiple_of(jnp.where(mine, core, 1 - core) * HALF, HALF), HALF)
@@ -159,12 +163,10 @@
         load_rows(0)
         load_rows(1)
         wait_columns(3, 4)
-        for unit in (2, 3, 4):
+        for unit in range(2, 8):
             load_rows(unit)
         for q in range(3):
             load_columns(q)
-        for unit in (5, 6, 7):
-            load_rows(unit)
     else:
         for q in range(3):
             load_columns(q)
@@ -172,18 +174,25 @@
             load_rows(unit)
         wait_columns(0, 3)
 
-    @pl.loop(0, 5)
-    def _(unit):
-        wait_rows(unit)
-        multiply(unit, *((3, 4) if late else (0, 3)))
-
     if late:
+        @pl.loop(0, 4)
+        def _(pair):
+            for n in range(2):
+                wait_rows(2 * pair + n)
+            result = product_of(iv[pl.ds(2 * pair, 2)].reshape(2 * HALF, 2 * depth), 3, 4)
+            for n in range(2):
+                multiply(2 * pair + n, 3, 4, result[n * HALF:(n + 1) * HALF])
+
         wait_columns(0, 3)
 
         @pl.loop(5, 8)
         def _(unit):
+            multiply(unit, 0, 3)
+    else:
+        @pl.loop(0, 5)
+        def _(unit):
             wait_rows(unit)
-            multiply(unit, 0, 4)
+            multiply(unit, 0, 3)
 
     if late:
         @pl.loop(5, 8)

time: 151 us -> 151 us (level)
  no operation moved by 1% of the time
where the time goes in v6:
time: 151 us
  blocking collectives  54.3 us (36%)
  waiting for transfers between devices  40.6 us (27%)
  Pallas kernels  37 us (25%)
  starting transfers between devices  16 us (11%)
  local copies, waits for them, and re-layouts  1.57 us (1%)
    all_to_all x1, blocking collectives, body(): lax.all_to_all(packed, AXES, 0, 0, tiled=True, axis_index_groups=groups)  54.3 us
    ppermute x11, waiting for transfers between devices, permute(): return lax.ppermute(a, AXES, pairs)  40.6 us
    pallas_call x2, Pallas kernels, product(): pl.pallas_call(lambda *refs: product_kernel(late, *refs), grid_spec=pltpu...  23.7 us
    ppermute x11, starting transfers between devices, permute(): return lax.ppermute(a, AXES, pairs)  16 us
    pallas_call x1, Pallas kernels, half_rows(): pl.pallas_call(half_kernel, grid_spec=pltpu.PrefetchScalarGridSpec(num_sc...  8.63 us
  transfers between devices with their start and end apart: 11, of which 7 were waited for; matrix products, arithmetic and copies ran while one was open for 1% of the time, Pallas kernels for 9%

profile of v6, /device:TPU:1, one launch (start us, length us, event | category | flops | bytes accessed | tf_op | source)
XLA Modules:
  0.0 150.5 jit_solution(1703009239294169198)
XLA Ops:
  0.7 8.6 %half_rows.1 = bf16[2,256,1536]{2,1,0:T(8,128)(2,1)} custom-call(s32[32]{0:T(128)} %rows_ref.1, s32[32]{0:T(128)} %cols_ref.1, s32[1]{0:T(128)S(6)} %copy.10.count_ref, bf16[32,24,4096]{2,1,0:T(8,128)(2,1)} %blocks_ref.1, bf16[64,8192]{1,0:T(8,128)(2,1)} %bitcast.5), custom_call_target="tpu_custom_call" | custom-call | flops 2000000000 | bytes 8000000 | tf_op jit(solution)/shard_map/half_rows/pallas_call | solution.py:82
  9.3 1.4 collective-permute-start
  10.7 1.5 fusion
  12.2 1.8 %collective-permute-done = bf16[2,256,1536]{2,1,0:T(8,128)(2,1)S(1)} collective-permute-done((bf16[2,256,1536]{2,1,0:T(8,128)(2,1)}, bf16[2,256,1536]{2,1,0:T(8,128)(2,1)S(1)}, u32[]{:S(2)}, u32[]{:S(2)}) %collective-permute-start) | collective-permute-done | bytes 1572896 | tf_op jit(solution)/shard_map/ppermute | solution.py:26
  14.0 0.1 fusion.1
  14.1 0.1 pad_maximum_fusion.refs_1_.refs_6_.refs_9_
  14.2 1.8 %collective-permute-start.1 = (bf16[2,256,1536]{2,1,0:T(8,128)(2,1)S(1)}, bf16[2,256,1536]{2,1,0:T(8,128)(2,1)}, u32[]{:S(2)}, u32[]{:S(2)}) collective-permute-start(bf16[2,256,1536]{2,1,0:T(8,128)(2,1)S(1)} %pad_maximum_fusion.refs_1_.refs_6_.refs_9_), channel_id=1, source_target_pairs={{0,24},{1,9},{2,26},{3,11},{4,28},{5,13},{6,30},{7,15},{8,0},{9,17... | collective-permute-start | bytes 4718600 | tf_op jit(solution)/shard_map/ppermute | solution.py:26
  16.0 1.3 collective-permute-start.6
  17.3 0.1 pad_maximum_fusion.1.refs_2_
  17.4 1.7 %collective-permute-start.3 = (bf16[2,256,1536]{2,1,0:T(8,128)(2,1)S(1)}, bf16[2,256,1536]{2,1,0:T(8,128)(2,1)}, u32[]{:S(2)}, u32[]{:S(2)}) collective-permute-start(bf16[2,256,1536]{2,1,0:T(8,128)(2,1)S(1)} %pad_maximum_fusion.1.refs_2_), channel_id=1, source_target_pairs={{0,24},{1,9},{2,26},{3,11},{4,28},{5,13},{6,30},{7,15},{8,0},{9,17... | collective-permute-start | bytes 4718600 | tf_op jit(solution)/shard_map/ppermute | solution.py:26
  19.2 1.9 %collective-permute-start.8 = (bf16[2,256,1536]{2,1,0:T(8,128)(2,1)S(1)}, bf16[2,256,1536]{2,1,0:T(8,128)(2,1)}, u32[]{:S(2)}, u32[]{:S(2)}) collective-permute-start(bf16[2,256,1536]{2,1,0:T(8,128)(2,1)S(1)} %pad_maximum_fusion.1.refs_2_), channel_id=1, source_target_pairs={{0,97},{1,32},{2,99},{3,34},{4,101},{5,36},{6,103},{7,38},{8,105},... | collective-permute-start | bytes 4718600 | tf_op jit(solution)/shard_map/ppermute | solution.py:26
  21.0 15.0 %collective-permute-done.1.refs_3_ = bf16[2,256,1536]{2,1,0:T(8,128)(2,1)} collective-permute-done((bf16[2,256,1536]{2,1,0:T(8,128)(2,1)S(1)}, bf16[2,256,1536]{2,1,0:T(8,128)(2,1)}, u32[]{:S(2)}, u32[]{:S(2)}) %collective-permute-start.1) | collective-permute-done | bytes 1572896 | tf_op jit(solution)/shard_map/ppermute | solution.py:26
  36.0 0.7 collective-permute-start.2
  36.7 0.0 collective-permute-done.6.refs_7_.refs_10_
  36.7 1.3 collective-permute-start.7
  38.0 0.6 collective-permute-start.5
  38.6 0.1 pad_add_fusion.refs_0_.place_ref
  38.7 14.5 %collective-permute-done.3.refs_5_ = bf16[2,256,1536]{2,1,0:T(8,128)(2,1)} collective-permute-done((bf16[2,256,1536]{2,1,0:T(8,128)(2,1)S(1)}, bf16[2,256,1536]{2,1,0:T(8,128)(2,1)}, u32[]{:S(2)}, u32[]{:S(2)}) %collective-permute-start.3) | collective-permute-done | bytes 1572896 | tf_op jit(solution)/shard_map/ppermute | solution.py:26
  53.2 0.4 collective-permute-start.4
  53.6 2.2 %collective-permute-done.8.refs_8_.refs_11_ = bf16[2,256,1536]{2,1,0:T(8,128)(2,1)} collective-permute-done((bf16[2,256,1536]{2,1,0:T(8,128)(2,1)S(1)}, bf16[2,256,1536]{2,1,0:T(8,128)(2,1)}, u32[]{:S(2)}, u32[]{:S(2)}) %collective-permute-start.8) | collective-permute-done | bytes 1572896 | tf_op jit(solution)/shard_map/ppermute | solution.py:26
  55.8 0.0 collective-permute-done.2.refs_4_
  55.8 11.1 %product_early.1.refs_13_ = bf16[16,2,512,128]{3,2,1,0:T(8,128)(2,1)S(1)} custom-call(s32[4]{0:T(128)S(1)} %pad_add_fusion.refs_0_.place_ref, bf16[2,256,1536]{2,1,0:T(8,128)(2,1)S(1)} %pad_maximum_fusion.refs_1_.refs_6_.refs_9_, bf16[2,256,1536]{2,1,0:T(8,128)(2,1)S(1)} %pad_maximum_fusion.1.refs_2_, bf16[2,256,1536]{2,1,0:T(8,128)(2,1)} %collective-permute-done.1.refs_3_, ...), custom_call_target="tpu_custom_call" | custom-call | flops 6039797760 | bytes 12582912 | tf_op jit(solution)/shard_map/product_early/pallas_call | solution.py:211
  66.9 3.5 %collective-permute-done.7.refs_12_ = bf16[2,256,1536]{2,1,0:T(8,128)(2,1)} collective-permute-done((bf16[2,256,1536]{2,1,0:T(8,128)(2,1)}, bf16[2,256,1536]{2,1,0:T(8,128)(2,1)}, u32[]{:S(2)}, u32[]{:S(2)}) %collective-permute-start.7) | collective-permute-done | bytes 1572896 | tf_op jit(solution)/shard_map/ppermute | solution.py:26
  70.4 0.0 collective-permute-done.5.refs_7_
  70.4 3.2 %collective-permute-start.9 = (bf16[2,256,1536]{2,1,0:T(8,128)(2,1)}, bf16[2,256,1536]{2,1,0:T(8,128)(2,1)S(1)}, u32[]{:S(2)}, u32[]{:S(2)}) collective-permute-start(bf16[2,256,1536]{2,1,0:T(8,128)(2,1)} %collective-permute-done.5.refs_7_), channel_id=1, source_target_pairs={{0,1},{1,0},{2,3},{3,2},{4,5},{5,4},{6,7},{7,6},{8,9},{9,8},{10,11... | collective-permute-start | bytes 4718600 | tf_op jit(solution)/shard_map/ppermute | solution.py:26
  73.5 0.0 collective-permute-done.4.refs_6_
  73.5 3.2 %collective-permute-done.9.refs_8_ = bf16[2,256,1536]{2,1,0:T(8,128)(2,1)S(1)} collective-permute-done((bf16[2,256,1536]{2,1,0:T(8,128)(2,1)}, bf16[2,256,1536]{2,1,0:T(8,128)(2,1)S(1)}, u32[]{:S(2)}, u32[]{:S(2)}) %collective-permute-start.9) | collective-permute-done | bytes 1572896 | tf_op jit(solution)/shard_map/ppermute | solution.py:26
  76.8 12.6 %product_late.1 = bf16[16,2,512,128]{3,2,1,0:T(8,128)(2,1)S(1)} custom-call(s32[4]{0:T(128)S(1)} %pad_add_fusion.refs_0_.place_ref, bf16[2,256,1536]{2,1,0:T(8,128)(2,1)S(1)} %pad_maximum_fusion.refs_1_.refs_6_.refs_9_, bf16[2,256,1536]{2,1,0:T(8,128)(2,1)S(1)} %pad_maximum_fusion.1.refs_2_, ...), custom_call_target="tpu_custom_call", output_to_operand_aliasing={{}: (13, {})} | custom-call | flops 6845104128 | bytes 18874368 | tf_op jit(solution)/shard_map/product_late/pallas_call | solution.py:211
  89.4 54.3 %all_to_all.5.parts = bf16[16,2,512,128]{3,2,1,0:T(8,128)(2,1)S(1)} all-to-all(bf16[16,2,512,128]{3,2,1,0:T(8,128)(2,1)S(1)} %product_late.1), channel_id=1, replica_groups={{0,2,4,6,8,10,12,14,16,18,20,22,24,26,28,30},{1,3,5,7,9,11,13,15,17,19,..., dimensions={0} | all-to-all | bytes 8388608 | tf_op jit(solution)/shard_map/all_to_all | solution.py:377
  143.7 1.1 sum_give.1
  144.9 1.7 %collective-permute-start.10 = (f32[2,2,512,128]{3,2,1,0:T(8,128)S(1)}, f32[2,2,512,128]{3,2,1,0:T(8,128)S(1)}, u32[]{:S(2)}, u32[]{:S(2)}) collective-permute-start(f32[2,2,512,128]{3,2,1,0:T(8,128)S(1)} %sum_give.1), channel_id=1, source_target_pairs={{0,1},{1,0},{2,3},{3,2},{4,5},{5,4},{6,7},{7,6},{8,9},{9,8},{10,11... | collective-permute-start | bytes 3145736 | tf_op jit(solution)/shard_map/ppermute | solution.py:26
  146.6 1.9 %sum_keep.1.before = f32[512,1024]{1,0:T(8,128)} custom-call(s32[4]{0:T(128)S(1)} %pad_add_fusion.refs_0_.place_ref, f32[1]{0:T(128)} %constant.16.clone.1.scale_ref, bf16[16,2,512,128]{3,2,1,0:T(8,128)(2,1)S(1)} %all_to_all.5.parts), custom_call_target="tpu_custom_call" | custom-call | flops 2097152 | bytes 6291456 | tf_op jit(solution)/shard_map/sum_keep/pallas_call | solution.py:287
  148.5 0.4 collective-permute-done.10.src
  148.9 1.6 %assemble.1 = f32[512,1024]{1,0:T(8,128)} custom-call(s32[4]{0:T(128)S(1)} %pad_add_fusion.refs_0_.place_ref, f32[2,2,512,128]{3,2,1,0:T(8,128)S(1)} %collective-permute-done.10.src, f32[512,1024]{1,0:T(8,128)} %sum_keep.1.before), custom_call_target="tpu_custom_call", output_to_operand_aliasing={{}: (2, {})} | custom-call | tf_op jit(solution)/shard_map/assemble/pallas_call | solution.py:325
Async XLA Ops:
  9.3 4.7 %collective-permute-start = (bf16[2,256,1536]{2,1,0:T(8,128)(2,1)}, bf16[2,256,1536]{2,1,0:T(8,128)(2,1)S(1)}, u32[]{:S(2)}, u32[]{:S(2)}) collective-permute-start(bf16[2,256,1536]{2,1,0:T(8,128)(2,1)} %half_rows.1), channel_id=1, source_target_pairs={{0,1},{1,0},{2,3},{3,2},{4,5},{5,4},{6,7},{7,6},{8,9},{9,8},{10,11... | collective-permute-start | bytes 4718600 | tf_op jit(solution)/shard_map/ppermute | solution.py:26
  14.2 21.8 %collective-permute-start.1 = (bf16[2,256,1536]{2,1,0:T(8,128)(2,1)S(1)}, bf16[2,256,1536]{2,1,0:T(8,128)(2,1)}, u32[]{:S(2)}, u32[]{:S(2)}) collective-permute-start(bf16[2,256,1536]{2,1,0:T(8,128)(2,1)S(1)} %pad_maximum_fusion.refs_1_.refs_6_.refs_9_), channel_id=1, source_target_pairs={{0,24},{1,9},{2,26},{3,11},{4,28},{5,13},{6,30},{7,15},{8,0},{9,17... | collective-permute-start | bytes 4718600 | tf_op jit(solution)/shard_map/ppermute | solution.py:26
  16.0 20.7 %collective-permute-start.6 = (bf16[2,256,1536]{2,1,0:T(8,128)(2,1)S(1)}, bf16[2,256,1536]{2,1,0:T(8,128)(2,1)}, u32[]{:S(2)}, u32[]{:S(2)}) collective-permute-start(bf16[2,256,1536]{2,1,0:T(8,128)(2,1)S(1)} %pad_maximum_fusion.refs_1_.refs_6_.refs_9_), channel_id=1, source_target_pairs={{0,96},{1,33},{2,98},{3,35},{4,100},{5,37},{6,102},{7,39},{8,104},... | collective-permute-start | bytes 4718600 | tf_op jit(solution)/shard_map/ppermute | solution.py:26
  17.4 35.7 %collective-permute-start.3 = (bf16[2,256,1536]{2,1,0:T(8,128)(2,1)S(1)}, bf16[2,256,1536]{2,1,0:T(8,128)(2,1)}, u32[]{:S(2)}, u32[]{:S(2)}) collective-permute-start(bf16[2,256,1536]{2,1,0:T(8,128)(2,1)S(1)} %pad_maximum_fusion.1.refs_2_), channel_id=1, source_target_pairs={{0,24},{1,9},{2,26},{3,11},{4,28},{5,13},{6,30},{7,15},{8,0},{9,17... | collective-permute-start | bytes 4718600 | tf_op jit(solution)/shard_map/ppermute | solution.py:26
  19.2 36.6 %collective-permute-start.8 = (bf16[2,256,1536]{2,1,0:T(8,128)(2,1)S(1)}, bf16[2,256,1536]{2,1,0:T(8,128)(2,1)}, u32[]{:S(2)}, u32[]{:S(2)}) collective-permute-start(bf16[2,256,1536]{2,1,0:T(8,128)(2,1)S(1)} %pad_maximum_fusion.1.refs_2_), channel_id=1, source_target_pairs={{0,97},{1,32},{2,99},{3,34},{4,101},{5,36},{6,103},{7,38},{8,105},... | collective-permute-start | bytes 4718600 | tf_op jit(solution)/shard_map/ppermute | solution.py:26
  36.0 19.7 %collective-permute-start.2 = (bf16[2,256,1536]{2,1,0:T(8,128)(2,1)}, bf16[2,256,1536]{2,1,0:T(8,128)(2,1)}, u32[]{:S(2)}, u32[]{:S(2)}) collective-permute-start(bf16[2,256,1536]{2,1,0:T(8,128)(2,1)} %collective-permute-done.1.refs_3_), channel_id=1, source_target_pairs={{0,1},{1,0},{2,3},{3,2},{4,5},{5,4},{6,7},{7,6},{8,9},{9,8},{10,11... | collective-permute-start | bytes 4718600 | tf_op jit(solution)/shard_map/ppermute | solution.py:26
  36.7 33.6 %collective-permute-start.7 = (bf16[2,256,1536]{2,1,0:T(8,128)(2,1)}, bf16[2,256,1536]{2,1,0:T(8,128)(2,1)}, u32[]{:S(2)}, u32[]{:S(2)}) collective-permute-start(bf16[2,256,1536]{2,1,0:T(8,128)(2,1)} %collective-permute-done.6.refs_7_.refs_10_), channel_id=1, source_target_pairs={{0,96},{1,33},{2,98},{3,35},{4,100},{5,37},{6,102},{7,39},{8,104},... | collective-permute-start | bytes 4718600 | tf_op jit(solution)/shard_map/ppermute | solution.py:26
  38.0 32.3 %collective-permute-start.5 = (bf16[2,256,1536]{2,1,0:T(8,128)(2,1)}, bf16[2,256,1536]{2,1,0:T(8,128)(2,1)}, u32[]{:S(2)}, u32[]{:S(2)}) collective-permute-start(bf16[2,256,1536]{2,1,0:T(8,128)(2,1)} %collective-permute-done.1.refs_3_), channel_id=1, source_target_pairs={{0,24},{1,9},{2,26},{3,11},{4,28},{5,13},{6,30},{7,15},{8,0},{9,17... | collective-permute-start | bytes 4718600 | tf_op jit(solution)/shard_map/ppermute | solution.py:26
  53.2 20.4 %collective-permute-start.4 = (bf16[2,256,1536]{2,1,0:T(8,128)(2,1)}, bf16[2,256,1536]{2,1,0:T(8,128)(2,1)S(1)}, u32[]{:S(2)}, u32[]{:S(2)}) collective-permute-start(bf16[2,256,1536]{2,1,0:T(8,128)(2,1)} %collective-permute-done.3.refs_5_), channel_id=1, source_target_pairs={{0,1},{1,0},{2,3},{3,2},{4,5},{5,4},{6,7},{7,6},{8,9},{9,8},{10,11... | collective-permute-start | bytes 4718600 | tf_op jit(solution)/shard_map/ppermute | solution.py:26
  70.4 6.4 %collective-permute-start.9 = (bf16[2,256,1536]{2,1,0:T(8,128)(2,1)}, bf16[2,256,1536]{2,1,0:T(8,128)(2,1)S(1)}, u32[]{:S(2)}, u32[]{:S(2)}) collective-permute-start(bf16[2,256,1536]{2,1,0:T(8,128)(2,1)} %collective-permute-done.5.refs_7_), channel_id=1, source_target_pairs={{0,1},{1,0},{2,3},{3,2},{4,5},{5,4},{6,7},{7,6},{8,9},{9,8},{10,11... | collective-permute-start | bytes 4718600 | tf_op jit(solution)/shard_map/ppermute | solution.py:26
  144.9 4.0 %collective-permute-start.10 = (f32[2,2,512,128]{3,2,1,0:T(8,128)S(1)}, f32[2,2,512,128]{3,2,1,0:T(8,128)S(1)}, u32[]{:S(2)}, u32[]{:S(2)}) collective-permute-start(f32[2,2,512,128]{3,2,1,0:T(8,128)S(1)} %sum_give.1), channel_id=1, source_target_pairs={{0,1},{1,0},{2,3},{3,2},{4,5},{5,4},{6,7},{7,6},{8,9},{9,8},{10,11... | collective-permute-start | bytes 3145736 | tf_op jit(solution)/shard_map/ppermute | solution.py:26
